TPU v7x, 32 devices: a whole 2x2x4 slice. The times are simulated.
32 devices in a mesh: groups: 2 (over x), tx: 16 (over z, y, core).
Axes of the slice: x: 2, y: 2, z: 4, core: 2. Of those that a mesh axis runs over, the one named last changes fastest.
Arguments:
- features: bfloat16 [384, 64, 128], P(('groups', 'tx')), parts along dimension 0, may hold values from -6 to 6
- nbr_table: int32 [384, 27], P(('groups', 'tx')), parts along dimension 0, may hold values from 0 to 20, as said below
- rim_slots: int32 [32, 8], P(('groups', 'tx')), parts along dimension 0, may hold values from 0 to 12, as said below
- w_first: bfloat16 [3456, 128], P('tx'), may hold values from -0.1875 to 0.1875
- w_second: bfloat16 [3456, 128], P('tx'), may hold values from -0.1875 to 0.1875
- cotangent: bfloat16 [384, 64, 128], P(('groups', 'tx')), parts along dimension 0, may hold values from -0.059814453 to 0.059814453
Outputs:
- out_map: bfloat16 [384, 64, 128], P(('groups', 'tx')), parts along dimension 0
- grad_first: float32 [6912, 128], P(('groups', 'tx')), parts along dimension 0
- grad_second: float32 [6912, 128], P(('groups', 'tx')), parts along dimension 0
There are 2 independent parts, one for each index of `groups`. A program takes and returns all parts, laid end to end along the dimension named above; an argument that names none is the same for every part. Nothing has to cross between parts.
Inputs may be any that keep to these rules, and one draw needn't show every extreme that they name: `nbr_table`: A tile's bricks lie in 3 brick rows of 2 by 2 positions; the map strips of tiles t and t+1 touch at t's last and t+1's first brick row. Entry q of an active slot names the brick at brick offset q: a slot of the same tile (0 to 11), 12+i for entry i of the previous tile's last-row list, 12 + 4+i for entry i of the next tile's first-row list, or 20 where that brick is inactive or outside the map; every entry of an empty slot is 20. Some tiles have all 12 slots active. `rim_slots`: each half lists the active bricks of that brick row in order of position, then 12 up to 4 entries; every tile has at least one active brick in its first and in its last brick row, and some tiles have 4 in both.
All inputs are finite; a program needn't handle non-finite values.
Results may differ from a plain program's by a relative error of at most 0.0049.
Values may be sent and summed in bfloat16 or wider, within the bound.
A program may use at most 64 MiB of HBM per device.

v0:
```python
import jax
import jax.numpy as jnp
import numpy as np
from jax import lax
from jax.sharding import PartitionSpec as P

BS = 4


def padded_2(x, sides, width):
    for axis, dim in sides:
        size, length = (lax.axis_size(axis), x.shape[dim])
        up = [(i, (i + 1) % size) for i in range(size - 1)]
        down = [(j, i) for i, j in up]
        last = lax.slice_in_dim(x, length - width, length, axis=dim)
        initial = lax.slice_in_dim(x, 0, width, axis=dim)
        before = lax.ppermute(last, axis, up)
        after = lax.ppermute(initial, axis, down)
        x = jnp.concatenate([before, x, after], axis=dim)
    return x


def brick_tables(side):
    coords = np.arange(side**3)
    first = coords // (side * side)
    second = coords // side % side
    third = coords % side
    brick_code = np.zeros((side**3, 27), np.int32)
    voxel_code = np.zeros((side**3, 27), np.int32)
    for offset in range(27):
        shifts = (offset // 9 - 1, offset // 3 % 3 - 1, offset % 3 - 1)
        code = np.zeros(side**3, np.int32)
        local = np.zeros(side**3, np.int32)
        for along, step in zip((first, second, third), shifts):
            moved = along + step
            brick_step = moved // side
            code = code * 3 + brick_step + 1
            local = local * side + moved - brick_step * side
        brick_code[:, offset] = code
        voxel_code[:, offset] = local
    return (brick_code, voxel_code)


def windows(extended, table, brick_code, voxel_code):
    vox_count = extended.shape[1]
    flat = extended.reshape(-1, extended.shape[2])
    index = table[:, brick_code] * vox_count + jnp.asarray(voxel_code)[None]
    picked = jnp.take(flat, index.reshape(-1).astype(jnp.int32), axis=0)
    return picked.reshape(table.shape[0] * vox_count, -1)


def on_device(features, nbr_table, rim_slots, w_first, w_second, cotangent):
    capacity, vox_count, channels = features.shape
    rim_count = rim_slots.shape[1] // 2
    brick_code, voxel_code = brick_tables(BS)
    zero_brick = jnp.zeros((1, vox_count, channels), jnp.bfloat16)
    own_lists = rim_slots[0]

    def extend(blocks):
        padded = jnp.concatenate([blocks, zero_brick], axis=0)
        packed = jnp.take(padded, own_lists, axis=0)
        beside_all = padded_2(packed, (("tx", 0),), rim_count)
        return jnp.concatenate(
            [blocks, beside_all[:rim_count], beside_all[3 * rim_count :], zero_brick], axis=0
        )

    inputs = windows(extend(features), nbr_table, brick_code, voxel_code)
    piece = lax.all_gather(w_first, "tx", axis=0, tiled=True)
    column_block = lax.slice_in_dim(inputs, 0, piece.shape[0], axis=1)
    first_sum = jnp.dot(column_block, piece, preferred_element_type=jnp.float32)
    hidden = jax.nn.silu(first_sum).astype(jnp.bfloat16)
    second_whole = lax.all_gather(w_second, "tx", axis=0, tiled=True)
    middle = windows(
        extend(hidden.reshape(capacity, vox_count, channels)), nbr_table, brick_code, voxel_code
    )
    out_map = jnp.dot(middle, second_whole, preferred_element_type=jnp.float32).astype(jnp.bfloat16)
    out_map = out_map.reshape(capacity, vox_count, channels)
    cot_rows = cotangent.reshape(-1, channels)
    contract = (((0,), (0,)), ((), ()))
    kernel_count = second_whole.shape[0] // channels
    flipped = (
        second_whole.reshape(kernel_count, channels, channels)[::-1]
        .transpose(0, 2, 1)
        .reshape(-1, channels)
    )
    back = jnp.dot(
        windows(extend(cotangent), nbr_table, brick_code, voxel_code),
        flipped,
        preferred_element_type=jnp.float32,
    )
    sigmoid_mid = jax.nn.sigmoid(first_sum)
    grad_mid = (back * sigmoid_mid * (1.0 + first_sum * (1.0 - sigmoid_mid))).astype(jnp.bfloat16)
    term_second = lax.dot_general(middle, cot_rows, contract, preferred_element_type=jnp.float32)
    term_first = lax.dot_general(inputs, grad_mid, contract, preferred_element_type=jnp.float32)
    grad_first, grad_second = (
        lax.psum_scatter(term_first, "tx", scatter_dimension=0, tiled=True),
        lax.psum_scatter(term_second, "tx", scatter_dimension=0, tiled=True),
    )
    return (out_map, grad_first, grad_second)


def solution(mesh):
    placed = (
        P(("groups", "tx"), None, None),
        P(("groups", "tx"), None),
        P(("groups", "tx"), None),
        P("tx", None),
        P("tx", None),
        P(("groups", "tx"), None, None),
    )
    return jax.shard_map(
        on_device,
        mesh=mesh,
        in_specs=placed,
        out_specs=(
            P(("groups", "tx"), None, None),
            P(("groups", "tx"), None),
            P(("groups", "tx"), None),
        ),
        check_vma=False,
    )
```

profile of v0, /device:TPU:0, one launch (start us, length us, event | category | flops | bytes accessed | tf_op | source)
XLA Modules:
  0.0 361.7 jit_solution(17203760057079737006)
XLA Ops:
  7.2 0.0 copy-start.5
  7.2 0.0 copy-start.3
  7.2 0.0 copy-start.4
  7.2 0.0 reduce-scatter.7.cloned.1.call-start
  7.2 0.7 compare_select_fusion.1
  7.9 0.7 compare_and_fusion.1
  8.6 0.9 concatenate.22
  9.5 0.9 concatenate.18
  10.5 0.6 gather_fusion.5
  11.1 0.6 gather_fusion.1
  11.6 0.1 broadcast_select_fusion.3
  11.7 0.7 fusion.10
  12.4 3.0 collective-permute-start
  15.4 1.3 collective-permute-start.1
  16.6 0.7 fusion.8
  17.3 5.2 %collective-permute-start.4 = (bf16[4,64,128]{2,1,0:T(8,128)(2,1)}, bf16[4,64,128]{2,1,0:T(8,128)(2,1)}, u32[]{:S(2)}, u32[]{:S(2)}) collective-permute-start(bf16[4,64,128]{2,1,0:T(8,128)(2,1)} %get-tuple-element.5), channel_id=1, source_target_pairs={{0,1},{1,2},{2,3},{3,4},{4,5},{5,6},{6,7},{7,8},{8,9},{9,10},{10,1... | collective-permute-start | bytes 196616 | tf_op jit(solution)/shard_map/ppermute | solution.py:17
  22.5 1.3 collective-permute-start.5
  23.8 0.8 copy.23
  24.6 0.7 pad_clamp_fusion.1
  25.3 3.3 gather_fusion
  28.5 0.0 copy-start
  28.5 0.3 copy.24
  28.9 0.4 reshape.143
  29.3 0.0 copy-done.5
  29.3 0.3 add.67
  29.6 0.6 compare_and_fusion
  30.2 0.7 pad_clamp_fusion
  30.9 0.0 copy-done.3
  30.9 27.3 %all_gather.6 = bf16[3456,128]{1,0:T(8,128)(2,1)} all-gather(bf16[216,128]{1,0:T(8,128)(2,1)S(1)} %copy-done.3), channel_id=1, replica_groups=mesh['groups'=2,'tx'=16] {'tx'}, dimensions={0}, use_global_device_ids=true | all-gather | bytes 940032 | tf_op jit(solution)/shard_map/all_gather | solution.py:68
  58.2 0.0 copy-done.4
  58.2 19.9 %all_gather.7 = bf16[3456,128]{1,0:T(8,128)(2,1)S(1)} all-gather(bf16[216,128]{1,0:T(8,128)(2,1)S(1)} %copy-done.4), channel_id=1, replica_groups=mesh['groups'=2,'tx'=16] {'tx'}, dimensions={0}, use_global_device_ids=true | all-gather | bytes 940032 | tf_op jit(solution)/shard_map/all_gather | solution.py:72
  78.1 0.1 reverse_bitcast_fusion
  78.2 1.3 copy.25
  79.5 0.1 pad.14.clone
  79.6 0.0 collective-permute-done
  79.6 0.0 collective-permute-done.1
  79.6 0.0 collective-permute-done.4
  79.6 0.0 collective-permute-done.5
  79.6 0.0 copy-done
  79.6 1.2 maximum_maximum_fusion.2
  80.8 0.0 copy-start.1
  80.8 45.9 %gather_fusion.6 = bf16[20736,128]{1,0:T(8,128)(2,1)} fusion(bf16[1344,128]{1,0:T(8,128)(2,1)S(1)} %bitcast.30, s32[21504]{0:T(1024)} %pad_clamp_fusion), kind=kCustom, calls=%fused_computation.5.clone | custom fusion | bytes 10699776 | tf_op jit(solution)/shard_map/jit(_take)/gather | solution.py:48
  126.8 42.0 %gather_fusion.2 = bf16[20736,128]{1,0:T(8,128)(2,1)} fusion(bf16[1344,128]{1,0:T(8,128)(2,1)S(1)} %bitcast.29, s32[21504]{0:T(1024)S(1)} %copy-done.1), kind=kCustom, calls=%fused_computation.1.clone | custom fusion | bytes 10699776 | tf_op jit(solution)/shard_map/jit(_take)/gather | solution.py:48
  168.8 12.7 %broadcast_select_fusion = (bf16[20736,128]{1,0:T(8,128)(2,1)}, bf16[20736,128]{1,0:T(8,128)(2,1)}) fusion(bf16[20736,128]{1,0:T(8,128)(2,1)} %gather_fusion.6, pred[20736]{0:T(1024)(128)(4,1)S(1)} %copy-done.2, bf16[20736,128]{1,0:T(8,128)(2,1)} %gather_fusion.2), kind=kLoop, calls=%fused_computation.7 | loop fusion | flops 5308416 | bytes 21254400 | tf_op jit(solution)/shard_map/jit(_take)/select_n | solution.py:48
  181.5 10.4 %reshape.69 = bf16[768,3456]{1,0:T(8,128)(2,1)} reshape(bf16[20736,128]{1,0:T(8,128)(2,1)} %get-tuple-element.12) | data formatting | bytes 10616832 | tf_op jit(solution)/shard_map/reshape | solution.py:49
  191.9 10.4 %reshape.75 = bf16[768,3456]{1,0:T(8,128)(2,1)} reshape(bf16[20736,128]{1,0:T(8,128)(2,1)} %get-tuple-element.11) | data formatting | bytes 10616832 | tf_op jit(solution)/shard_map/reshape | solution.py:49
  202.3 4.3 %multiply_convert_fusion = (bf16[768,128]{1,0:T(8,128)(2,1)S(1)}, f32[768,128]{1,0:T(8,128)S(1)}) fusion(bf16[768,3456]{1,0:T(8,128)(2,1)} %reshape.69, bf16[3456,128]{1,0:T(8,128)(2,1)} %all_gather.6), kind=kOutput, calls=%fused_computation.20 | convolution fusion | flops 679968768 | bytes 6782976 | tf_op jit(solution)/shard_map/dot_general | solution.py:70
  206.7 0.6 gather_fusion.3
  207.2 0.1 broadcast_select_fusion.4
  207.4 2.3 collective-permute-start.2
  209.6 1.5 collective-permute-start.3
  211.1 10.7 %fusion.2 = f32[3456,128]{1,0:T(8,128)} fusion(bf16[768,3456]{1,0:T(8,128)(2,1)} %reshape.69, bf16[768,3456]{1,0:T(8,128)(2,1)} %reshape.75, bf16[3456,128]{1,0:T(8,128)(2,1)S(1)} %bitcast.33, f32[768,128]{1,0:T(8,128)S(1)} %get-tuple-element.18), kind=kOutput, calls=%fused_computation.15 | convolution fusion | flops 1359839232 | bytes 13664256 | tf_op jit(solution)/shard_map/dot_general | solution.py:94
  221.9 0.0 reduce-scatter.7.cloned.1.call-update
  221.9 0.0 reduce-scatter.9.cloned.1.call-start
  221.9 0.0 collective-permute-done.2
  221.9 0.0 collective-permute-done.3
  221.9 0.1 maximum_maximum_fusion.1
  222.0 42.0 %gather_fusion.4 = bf16[20736,128]{1,0:T(8,128)(2,1)} fusion(bf16[1344,128]{1,0:T(8,128)(2,1)S(1)} %bitcast.31, s32[21504]{0:T(1024)S(1)} %copy-done.1), kind=kCustom, calls=%fused_computation.4.clone | custom fusion | bytes 10699776 | tf_op jit(solution)/shard_map/jit(_take)/gather | solution.py:48
  264.1 13.9 %broadcast_select_fusion.2 = bf16[20736,128]{1,0:T(8,128)(2,1)} fusion(bf16[20736,128]{1,0:T(8,128)(2,1)} %gather_fusion.4, pred[20736]{0:T(1024)(128)(4,1)S(1)} %copy-done.2), kind=kLoop, calls=%fused_computation.9 | loop fusion | flops 2654208 | bytes 10637568 | tf_op jit(solution)/shard_map/jit(_take)/select_n | solution.py:48
  278.0 10.4 %reshape.72 = bf16[768,3456]{1,0:T(8,128)(2,1)} reshape(bf16[20736,128]{1,0:T(8,128)(2,1)} %broadcast_select_fusion.2) | data formatting | bytes 10616832 | tf_op jit(solution)/shard_map/reshape | solution.py:49
  288.4 5.3 %fusion.11 = f32[3456,128]{1,0:T(8,128)} fusion(bf16[768,3456]{1,0:T(8,128)(2,1)} %reshape.72, bf16[768,128]{1,0:T(8,128)(2,1)S(1)} %bitcast.34), kind=kOutput, calls=%fused_computation.41 | convolution fusion | flops 679477248 | bytes 7274496 | tf_op jit(solution)/shard_map/dot_general | solution.py:93
  293.7 0.0 reduce-scatter.9.cloned.1.call-update
  293.8 4.7 %convolution_convert_fusion = bf16[768,128]{1,0:T(8,128)(2,1)} fusion(bf16[768,3456]{1,0:T(8,128)(2,1)} %reshape.72, bf16[3456,128]{1,0:T(8,128)(2,1)S(1)} %all_gather.7), kind=kOutput, calls=%fused_computation.13 | convolution fusion | flops 679575552 | bytes 6389760 | tf_op jit(solution)/shard_map/dot_general | solution.py:76
  298.5 56.3 %reduce-scatter.9.cloned.1.call-done = f32[216,128]{1,0:T(8,128)} async-done(((f32[3456,128]{1,0:T(8,128)}), f32[216,128]{1,0:T(8,128)}) %reduce-scatter.9.cloned.1.call-update) | async-done | bytes 110608
  (10 shorter events, 0.1 us)
Async XLA Ops:
  7.2 22.1 %copy-start.5 = (s32[64,27]{1,0:T(8,128)S(1)}, s32[64,27]{1,0:T(8,128)}, u32[]{:S(2)}) copy-start(s32[64,27]{1,0:T(8,128)} %constant.22.clone) | copy-start | bytes 20740
  7.2 23.7 %copy-start.3 = (bf16[216,128]{1,0:T(8,128)(2,1)S(1)}, bf16[216,128]{1,0:T(8,128)(2,1)}, u32[]{:S(2)}) copy-start(bf16[216,128]{1,0:T(8,128)(2,1)} %param.18) | copy-start | bytes 165892
  7.2 51.0 %copy-start.4 = (bf16[216,128]{1,0:T(8,128)(2,1)S(1)}, bf16[216,128]{1,0:T(8,128)(2,1)}, u32[]{:S(2)}) copy-start(bf16[216,128]{1,0:T(8,128)(2,1)} %param.19) | copy-start | bytes 165892
  7.2 291.3 %reduce-scatter.7.cloned.1.call-start = ((), (), s32[]{:S(2)}) async-start(), calls=%async_computation.2 | async-start | bytes 1880064
  12.4 67.2 %collective-permute-start = (bf16[4,64,128]{2,1,0:T(8,128)(2,1)}, bf16[4,64,128]{2,1,0:T(8,128)(2,1)}, u32[]{:S(2)}, u32[]{:S(2)}) collective-permute-start(bf16[4,64,128]{2,1,0:T(8,128)(2,1)} %get-tuple-element.9), channel_id=1, source_target_pairs={{0,1},{1,2},{2,3},{3,4},{4,5},{5,6},{6,7},{7,8},{8,9},{9,10},{10,1... | collective-permute-start | bytes 196616 | tf_op jit(solution)/shard_map/ppermute | solution.py:17
  15.4 64.3 %collective-permute-start.1 = (bf16[4,64,128]{2,1,0:T(8,128)(2,1)}, bf16[4,64,128]{2,1,0:T(8,128)(2,1)}, u32[]{:S(2)}, u32[]{:S(2)}) collective-permute-start(bf16[4,64,128]{2,1,0:T(8,128)(2,1)} %get-tuple-element.10), channel_id=1, source_target_pairs={{1,0},{2,1},{3,2},{4,3},{5,4},{6,5},{7,6},{8,7},{9,8},{10,9},{11,1... | collective-permute-start | bytes 196616 | tf_op jit(solution)/shard_map/ppermute | solution.py:18
  17.3 62.3 %collective-permute-start.4 = (bf16[4,64,128]{2,1,0:T(8,128)(2,1)}, bf16[4,64,128]{2,1,0:T(8,128)(2,1)}, u32[]{:S(2)}, u32[]{:S(2)}) collective-permute-start(bf16[4,64,128]{2,1,0:T(8,128)(2,1)} %get-tuple-element.5), channel_id=1, source_target_pairs={{0,1},{1,2},{2,3},{3,4},{4,5},{5,6},{6,7},{7,8},{8,9},{9,10},{10,1... | collective-permute-start | bytes 196616 | tf_op jit(solution)/shard_map/ppermute | solution.py:17
  22.5 57.1 %collective-permute-start.5 = (bf16[4,64,128]{2,1,0:T(8,128)(2,1)}, bf16[4,64,128]{2,1,0:T(8,128)(2,1)}, u32[]{:S(2)}, u32[]{:S(2)}) collective-permute-start(bf16[4,64,128]{2,1,0:T(8,128)(2,1)} %get-tuple-element.6), channel_id=1, source_target_pairs={{1,0},{2,1},{3,2},{4,3},{5,4},{6,5},{7,6},{8,7},{9,8},{10,9},{11,1... | collective-permute-start | bytes 196616 | tf_op jit(solution)/shard_map/ppermute | solution.py:18
  28.5 51.1 %copy-start = (bf16[12,64,128]{2,1,0:T(8,128)(2,1)S(1)}, bf16[12,64,128]{2,1,0:T(8,128)(2,1)}, u32[]{:S(2)}) copy-start(bf16[12,64,128]{2,1,0:T(8,128)(2,1)} %param.20) | copy-start | bytes 589828
  80.8 46.0 %copy-start.1 = (s32[21504]{0:T(1024)S(1)}, s32[21504]{0:T(1024)}, u32[]{:S(2)}) copy-start(s32[21504]{0:T(1024)} %pad_clamp_fusion) | copy-start | bytes 258052
  126.8 42.1 %copy-start.2 = (pred[20736]{0:T(1024)(128)(4,1)S(1)}, pred[20736]{0:T(1024)(128)(4,1)}, u32[]{:S(2)}) copy-start(pred[20736]{0:T(1024)(128)(4,1)} %compare_and_fusion) | copy-start | bytes 62212
  207.4 14.6 %collective-permute-start.2 = (bf16[4,64,128]{2,1,0:T(8,128)(2,1)S(1)}, bf16[4,64,128]{2,1,0:T(8,128)(2,1)S(1)}, u32[]{:S(2)}, u32[]{:S(2)}) collective-permute-start(bf16[4,64,128]{2,1,0:T(8,128)(2,1)S(1)} %get-tuple-element.7), channel_id=1, source_target_pairs={{0,1},{1,2},{2,3},{3,4},{4,5},{5,6},{6,7},{7,8},{8,9},{9,10},{10,1... | collective-permute-start | bytes 196616 | tf_op jit(solution)/shard_map/ppermute | solution.py:17
  209.6 12.3 %collective-permute-start.3 = (bf16[4,64,128]{2,1,0:T(8,128)(2,1)S(1)}, bf16[4,64,128]{2,1,0:T(8,128)(2,1)S(1)}, u32[]{:S(2)}, u32[]{:S(2)}) collective-permute-start(bf16[4,64,128]{2,1,0:T(8,128)(2,1)S(1)} %get-tuple-element.8), channel_id=1, source_target_pairs={{1,0},{2,1},{3,2},{4,3},{5,4},{6,5},{7,6},{8,7},{9,8},{10,9},{11,1... | collective-permute-start | bytes 196616 | tf_op jit(solution)/shard_map/ppermute | solution.py:18
  221.9 132.9 %reduce-scatter.9.cloned.1.call-start = ((), (), s32[]{:S(2)}) async-start(), calls=%async_computation.3 | async-start | bytes 1880064
Sparse Core Ops, SparseCore 0:
  222.0 60.9 reduce-scatter.6
  293.9 60.8 reduce-scatter.8
where the time goes:
time: 365 us; the launch traced here: 362 us
  local copies, waits for them, and re-layouts  173 us (47%)
  waiting for transfers between devices  56.4 us (15%)
  blocking collectives  47.2 us (13%)
  other arithmetic  31.4 us (9%)
  matrix products  25.1 us (7%)
  starting transfers between devices  14.5 us (4%)
  between operations  14.3 us (4%)
    gather x3, local copies, waits for them, and re-layouts, windows(): picked = jnp.take(flat, index.reshape(-1).astype(jnp.int32), axis=0)  130 us
    unnamed x4, waiting for transfers between devices  56.4 us
    reshape x3, local copies, waits for them, and re-layouts, windows(): return picked.reshape(table.shape[0] * vox_count, -1)  31.3 us
    all_gather x1, blocking collectives, on_device(): piece = lax.all_gather(w_first, 'tx', axis=0, tiled=True)  27.3 us
    select_n x3, other arithmetic, windows(): picked = jnp.take(flat, index.reshape(-1).astype(jnp.int32), axis=0)  26.5 us
    all_gather x1, blocking collectives, on_device(): second_whole = lax.all_gather(w_second, 'tx', axis=0, tiled=True)  19.9 us
    dot_general x1, matrix products, on_device(): lax.dot_general(inputs, grad_mid, contract, preferred_element_type=jnp.fl...  10.7 us
    ppermute x3, starting transfers between devices, padded_2(): before = lax.ppermute(last, axis, up)  10.4 us
  transfers between devices with their start and end apart: 8, of which 1 were waited for; matrix products, arithmetic and copies ran while one was open for 27% of the time, Pallas kernels for 0%

commit v1 on v0

v1 whole, which is shorter than its diff:
```python
import jax
import jax.numpy as jnp
import numpy as np
from jax import lax
from jax.sharding import PartitionSpec as P

BS = 4
SLOTS = 16


def halo_tables(side):
    wide = side + 2
    coords = np.arange(wide**3)
    brick = np.zeros(wide**3, np.int32)
    local = np.zeros(wide**3, np.int32)
    for along in (coords // (wide * wide), coords // wide % wide, coords % wide):
        moved = along - 1
        step = moved // side
        brick = brick * 3 + step + 1
        local = local * side + moved - step * side
    return (brick.astype(np.int32), local.astype(np.int32))


def neighbours(packed, rim_count):
    size = lax.axis_size("tx")
    up = [(i, (i + 1) % size) for i in range(size - 1)]
    down = [(j, i) for i, j in up]
    before = lax.ppermute(packed[:, rim_count:], "tx", up)
    after = lax.ppermute(packed[:, :rim_count], "tx", down)
    return (before, after)


def on_device(features, nbr_table, rim_slots, w_first, w_second, cotangent):
    capacity, vox_count, channels = features.shape
    rim_count = rim_slots.shape[1] // 2
    chosen = rim_slots[0][:, None] == jnp.arange(capacity)[None, :]
    zero_slot = capacity + 2 * rim_count
    width = zero_slot + 4
    brick, local = halo_tables(BS)

    both_w = lax.all_gather(
        jnp.concatenate([w_first, w_second], axis=1), "tx", axis=0, tiled=True
    )

    table = jnp.pad(
        nbr_table, ((0, SLOTS - capacity), (0, 0)), constant_values=zero_slot
    ).T
    index = (jnp.take(table, brick, axis=0) + jnp.asarray(local)[:, None] * width).reshape(-1)

    def halo(blocks):
        live = blocks[:, :capacity]
        packed = jnp.sum(
            jnp.where(chosen[None, :, :, None], live[:, None], 0), axis=2, dtype=jnp.float32
        ).astype(blocks.dtype)
        before, after = neighbours(packed, rim_count)
        extended = jnp.concatenate(
            [
                live,
                before,
                after,
                jnp.zeros((vox_count, width - zero_slot, blocks.shape[2]), blocks.dtype),
            ],
            axis=1,
        )
        picked = jnp.take(
            extended.reshape(-1, blocks.shape[2]), index, axis=0, mode="clip"
        )
        wide = BS + 2
        return picked.reshape(wide, wide, wide, SLOTS, blocks.shape[2])

    def windows(padded):
        parts = []
        for offset in range(27):
            a, b, c = (offset // 9, offset // 3 % 3, offset % 3)
            part = padded[a : a + BS, b : b + BS, c : c + BS]
            parts.append(part.reshape(vox_count * SLOTS, channels))
        return jnp.concatenate(parts, axis=1)

    stacked = jnp.concatenate([features, cotangent], axis=2).transpose(1, 0, 2)
    outer = halo(stacked)
    inputs = windows(outer[..., :channels])
    cots = windows(outer[..., channels:])
    full_first, full_second = (both_w[:, :channels], both_w[:, channels:])
    kernel_count = full_second.shape[0] // channels
    flipped = (
        full_second.reshape(kernel_count, channels, channels)[::-1]
        .transpose(0, 2, 1)
        .reshape(-1, channels)
    )
    first_sum = jnp.dot(inputs, full_first, preferred_element_type=jnp.float32)
    sigmoid_mid = jax.nn.sigmoid(first_sum)
    hidden = (first_sum * sigmoid_mid).astype(jnp.bfloat16)
    back = jnp.dot(cots, flipped, preferred_element_type=jnp.float32)
    grad_mid = (back * sigmoid_mid * (1.0 + first_sum * (1.0 - sigmoid_mid))).astype(jnp.bfloat16)
    contract = (((0,), (0,)), ((), ()))
    term_first = lax.dot_general(inputs, grad_mid, contract, preferred_element_type=jnp.float32)
    grad_first = lax.psum_scatter(term_first, "tx", scatter_dimension=0, tiled=True)

    middle = windows(halo(hidden.reshape(vox_count, SLOTS, channels)))
    out_map = jnp.dot(middle, full_second, preferred_element_type=jnp.float32).astype(jnp.bfloat16)
    out_map = out_map.reshape(vox_count, SLOTS, channels)[:, :capacity].transpose(1, 0, 2)
    cot_rows = jnp.pad(
        stacked[..., channels:], ((0, 0), (0, SLOTS - capacity), (0, 0))
    ).reshape(-1, channels)
    term_second = lax.dot_general(middle, cot_rows, contract, preferred_element_type=jnp.float32)
    grad_second = lax.psum_scatter(term_second, "tx", scatter_dimension=0, tiled=True)
    return (out_map, grad_first, grad_second)


def solution(mesh):
    placed = (
        P(("groups", "tx"), None, None),
        P(("groups", "tx"), None),
        P(("groups", "tx"), None),
        P("tx", None),
        P("tx", None),
        P(("groups", "tx"), None, None),
    )
    return jax.shard_map(
        on_device,
        mesh=mesh,
        in_specs=placed,
        out_specs=(
            P(("groups", "tx"), None, None),
            P(("groups", "tx"), None),
            P(("groups", "tx"), None),
        ),
        check_vma=False,
    )
```

time: 365 us -> 219 us (0.60)
  local copies, waits for them, and re-layouts: 173 us -> 57.9 us
  waiting for transfers between devices: 56.4 us -> 108 us
  blocking collectives: 47.2 us -> 0 us
  other arithmetic: 31.4 us -> 5.54 us
  starting transfers between devices: 14.5 us -> 7.42 us
    gather x8 -> x3, local copies, waits for them, and re-layouts: 135 us -> 18.5 us  [the longest x2 17.8 us: halo(): jnp.take(extended.reshape(-1, blocks.shape[2]), index, axis=0, mode='clip')]
    unnamed x4 -> x5, waiting for transfers between devices: 56.4 us -> 104 us
    all_gather x2 -> x0, blocking collectives: 47.2 us -> none  [the longest x1 27.3 us: on_device(): piece = lax.all_gather(w_first, 'tx', axis=0, tiled=True)]
    reshape x3 -> x0, local copies, waits for them, and re-layouts: 31.3 us -> none  [windows(): return picked.reshape(table.shape[0] * vox_count, -1)]
    unnamed x13 -> x88, local copies, waits for them, and re-layouts: 0.82 us -> 30.5 us
    select_n x6 -> x0, other arithmetic: 27.4 us -> none  [the longest x3 26.5 us: windows(): picked = jnp.take(flat, index.reshape(-1).astype(jnp.int32), axis=0)]
    ppermute x6 -> x4, starting transfers between devices: 14.4 us -> 7.3 us  [the longest x2 4.53 us: neighbours(): before = lax.ppermute(packed[:, rim_count:], 'tx', up)]
    dot_general x2 -> x3, matrix products: 9.01 us -> 15.4 us  [the longest x1 5.19 us: on_device(): first_sum = jnp.dot(inputs, full_first, preferred_element_type=jnp.float32)]
  transfers between devices with their start and end apart: 8 -> 7, of which waited for: 1 -> 3; matrix products, arithmetic and copies ran while one was open for 27% -> 34% of each run, Pallas kernels for 0% -> 0%
where the time goes in v1:
time: 219 us
  waiting for transfers between devices  108 us (49%)
  local copies, waits for them, and re-layouts  57.9 us (26%)
  matrix products  25 us (11%)
  between operations  14.5 us (7%)
  starting transfers between devices  7.42 us (3%)
  other arithmetic  5.54 us (3%)
    unnamed x5, waiting for transfers between devices  104 us
    unnamed x88, local copies, waits for them, and re-layouts  30.5 us
    gather x2, local copies, waits for them, and re-layouts, halo(): jnp.take(extended.reshape(-1, blocks.shape[2]), index, axis=0, mode='clip')  17.8 us
    dot_general x1, matrix products, on_device(): lax.dot_general(inputs, grad_mid, contract, preferred_element_type=jnp.fl...  6.25 us
    dot_general x1, matrix products, on_device(): first_sum = jnp.dot(inputs, full_first, preferred_element_type=jnp.float32)  5.19 us
    dot_general x1, matrix products, on_device(): jnp.dot(middle, full_second, preferred_element_type=jnp.float32)  5.15 us
    slice x5, local copies, waits for them, and re-layouts, windows(): part = padded[a:a + BS, b:b + BS, c:c + BS]  5.05 us
    dot_general x1, matrix products, on_device(): back = jnp.dot(cots, flipped, preferred_element_type=jnp.float32)  5.04 us
  transfers between devices with their start and end apart: 7, of which 3 were waited for; matrix products, arithmetic and copies ran while one was open for 34% of the time, Pallas kernels for 0%

profile of v1, /device:TPU:0, one launch (start us, length us, event | category | flops | bytes accessed | tf_op | source)
XLA Modules:
  0.0 218.5 jit_solution(14762262638874158919)
XLA Ops:
  7.2 1.1 copy.29
  8.3 1.1 copy.30
  9.3 0.7 iota_compare_fusion
  10.0 0.1 maximum_bitcast_fusion
  10.1 0.6 select_reduce_fusion
  10.8 2.4 %collective-permute-start = (bf16[64,4,256]{2,1,0:T(4,128)(2,1)S(1)}, bf16[64,4,256]{2,1,0:T(4,128)(2,1)S(1)}, u32[]{:S(2)}, u32[]{:S(2)}) collective-permute-start(bf16[64,4,256]{2,1,0:T(4,128)(2,1)S(1)} %get-tuple-element.84), channel_id=1, source_target_pairs={{0,1},{1,2},{2,3},{3,4},{4,5},{5,6},{6,7},{7,8},{8,9},{9,10},{10,1... | collective-permute-start | bytes 393224 | tf_op jit(solution)/shard_map/ppermute | solution.py:28
  13.2 1.3 collective-permute-start.1
  14.5 1.5 pad_maximum_fusion
  16.1 0.8 copy.31
  16.9 0.7 pad_clamp_fusion.1
  17.6 0.7 gather_fusion
  18.3 0.8 broadcast_add_fusion
  19.1 0.1 reshape.444
  19.4 0.5 maximum_maximum_fusion
  19.9 10.6 %gather_fusion.1 = bf16[3456,256]{1,0:T(8,128)(2,1)S(1)} fusion(bf16[1536,256]{1,0:T(8,128)(2,1)S(1)} %bitcast.111, s32[4096]{0:T(1024)S(1)} %pad_clamp_fusion), kind=kCustom, calls=%fused_computation.1 | custom fusion | bytes 3552768 | tf_op jit(solution)/shard_map/jit(_take)/gather | solution.py:65
  30.5 1.3 fusion.6
  31.8 1.3 fusion.5
  33.1 0.8 fusion.7
  34.0 0.7 constant_dynamic-update-slice_fusion.26
  36.6 0.8 constant_dynamic-update-slice_fusion.25
  37.4 1.2 constant_dynamic-update-slice_fusion.24
  38.6 1.1 constant_dynamic-update-slice_fusion.23
  39.7 0.7 constant_dynamic-update-slice_fusion.22
  40.4 0.8 constant_dynamic-update-slice_fusion.21
  41.2 0.8 constant_dynamic-update-slice_fusion.20
  42.0 0.8 constant_dynamic-update-slice_fusion.19
  42.8 0.7 constant_dynamic-update-slice_fusion.18
  43.5 0.7 constant_dynamic-update-slice_fusion.17
  44.2 0.8 constant_dynamic-update-slice_fusion.16
  45.0 0.8 constant_dynamic-update-slice_fusion.15
  45.8 0.8 constant_dynamic-update-slice_fusion.14
  46.5 0.8 constant_dynamic-update-slice_fusion.13
  47.3 0.8 constant_dynamic-update-slice_fusion.12
  48.1 0.8 constant_dynamic-update-slice_fusion.11
  48.9 0.8 constant_dynamic-update-slice_fusion.10
  49.7 0.7 constant_dynamic-update-slice_fusion.9
  50.4 0.8 constant_dynamic-update-slice_fusion.8
  51.2 0.7 constant_dynamic-update-slice_fusion.7
  51.9 0.8 constant_dynamic-update-slice_fusion.6
  52.7 0.7 constant_dynamic-update-slice_fusion.5
  53.4 0.8 constant_dynamic-update-slice_fusion.4
  54.2 0.8 constant_dynamic-update-slice_fusion.3
  54.9 0.7 constant_dynamic-update-slice_fusion.2
  55.7 0.8 constant_dynamic-update-slice_fusion.1
  56.4 0.7 constant_dynamic-update-slice_fusion
  57.2 4.0 %all-gather.2.cloned.1.call-done = bf16[3456,256]{1,0:T(8,128)(2,1)} async-done(((bf16[216,256]{1,0:T(8,128)(2,1)}), bf16[3456,256]{1,0:T(8,128)(2,1)}) %all-gather.2.cloned.1.call-update) | async-done | bytes 1769488 | tf_op jit(solution)/shard_map/all_gather | solution.py:41
  61.1 1.2 slice.482
  62.4 1.3 copy.33
  63.8 5.2 %multiply_convert_fusion = (bf16[1024,128]{1,0:T(8,128)(2,1)S(1)}, f32[1024,128]{1,0:T(8,128)S(1)}) fusion(bf16[1024,3456]{1,0:T(8,128)(2,1)} %constant_dynamic-update-slice_fusion, bf16[3456,256]{1,0:T(8,128)(2,1)} %all-gather.2.cloned.1.call-done), kind=kOutput, calls=%fused_computation.14 | convolution fusion | flops 906625024 | bytes 8749056 | tf_op jit(solution)/shard_map/dot_general | solution.py:90
  69.0 0.5 select_reduce_fusion.1
  69.5 2.2 collective-permute-start.2
  71.7 1.5 collective-permute-start.3
  73.2 5.0 %fusion.1 = bf16[1024,128]{1,0:T(8,128)(2,1)S(1)} fusion(bf16[1024,3456]{1,0:T(8,128)(2,1)} %copy-done.2, bf16[3456,128]{1,0:T(8,128)(2,1)S(1)} %bitcast.203, f32[1024,128]{1,0:T(8,128)S(1)} %get-tuple-element.89), kind=kOutput, calls=%fused_computation.7 | convolution fusion | flops 907149312 | bytes 8749056 | tf_op jit(solution)/shard_map/dot_general | solution.py:93
  78.2 6.2 %fusion.12 = f32[3456,128]{1,0:T(8,128)} fusion(bf16[1024,3456]{1,0:T(8,128)(2,1)} %constant_dynamic-update-slice_fusion, bf16[1024,128]{1,0:T(8,128)(2,1)S(1)} %fusion.1), kind=kOutput, calls=%fused_computation.113 | convolution fusion | flops 905969664 | bytes 9109504 | tf_op jit(solution)/shard_map/dot_general | solution.py:96
  84.6 0.2 maximum_maximum_fusion.1
  84.8 7.1 %gather_fusion.2 = bf16[3456,128]{1,0:T(8,128)(2,1)S(1)} fusion(bf16[1536,128]{1,0:T(8,128)(2,1)S(1)} %bitcast.115, s32[4096]{0:T(1024)S(1)} %pad_clamp_fusion), kind=kCustom, calls=%fused_computation.2 | custom fusion | bytes 1783296 | tf_op jit(solution)/shard_map/jit(_take)/gather | solution.py:65
  91.9 0.4 fusion.9
  92.3 1.3 fusion.8
  95.6 2.9 %copy-done = bf16[1024,3456]{1,0:T(8,128)(2,1)} copy-done((bf16[1024,3456]{1,0:T(8,128)(2,1)}, bf16[1024,3456]{1,0:T(8,128)(2,1)S(1)}, u32[]{:S(2)}) %copy-start) | copy-done | bytes 7077912
  98.5 3.4 %fusion.13 = f32[3456,128]{1,0:T(8,128)} fusion(bf16[1024,3456]{1,0:T(8,128)(2,1)S(1)} %constant_dynamic-update-slice_fusion.27, bf16[1024,128]{1,0:T(8,128)(2,1)S(1)} %bitcast.119), kind=kOutput, calls=%fused_computation.114 | convolution fusion | flops 905969664 | bytes 9109504 | tf_op jit(solution)/shard_map/dot_general | solution.py:105
  101.9 5.2 %convolution_convert_fusion = bf16[1024,128]{1,0:T(8,128)(2,1)S(1)} fusion(bf16[1024,3456]{1,0:T(8,128)(2,1)} %copy-done, bf16[3456,256]{1,0:T(8,128)(2,1)S(1)} %copy-done.1), kind=kOutput, calls=%fused_computation.8 | convolution fusion | flops 906100736 | bytes 8224768 | tf_op jit(solution)/shard_map/dot_general | solution.py:100
  107.1 0.7 copy.36
  107.8 40.7 %reduce-scatter.7.cloned.1.call-done = f32[216,128]{1,0:T(8,128)} async-done(((f32[3456,128]{1,0:T(8,128)}), f32[216,128]{1,0:T(8,128)}) %reduce-scatter.7.cloned.1.call-update) | async-done | bytes 110608
  148.5 63.5 %reduce-scatter.9.cloned.1.call-done = f32[216,128]{1,0:T(8,128)} async-done(((f32[3456,128]{1,0:T(8,128)}), f32[216,128]{1,0:T(8,128)}) %reduce-scatter.9.cloned.1.call-update) | async-done | bytes 110608
  (78 shorter events, 4.0 us)
Async XLA Ops:
  7.2 54.0 %all-gather.2.cloned.1.call-start = ((), (), s32[]{:S(2)}) async-start(), calls=%async_computation.2 | async-start | bytes 1880064 | tf_op jit(solution)/shard_map/all_gather | solution.py:41
  10.8 8.5 %collective-permute-start = (bf16[64,4,256]{2,1,0:T(4,128)(2,1)S(1)}, bf16[64,4,256]{2,1,0:T(4,128)(2,1)S(1)}, u32[]{:S(2)}, u32[]{:S(2)}) collective-permute-start(bf16[64,4,256]{2,1,0:T(4,128)(2,1)S(1)} %get-tuple-element.84), channel_id=1, source_target_pairs={{0,1},{1,2},{2,3},{3,4},{4,5},{5,6},{6,7},{7,8},{8,9},{9,10},{10,1... | collective-permute-start | bytes 393224 | tf_op jit(solution)/shard_map/ppermute | solution.py:28
  13.2 6.2 %collective-permute-start.1 = (bf16[64,4,256]{2,1,0:T(4,128)(2,1)S(1)}, bf16[64,4,256]{2,1,0:T(4,128)(2,1)S(1)}, u32[]{:S(2)}, u32[]{:S(2)}) collective-permute-start(bf16[64,4,256]{2,1,0:T(4,128)(2,1)S(1)} %get-tuple-element.85), channel_id=1, source_target_pairs={{1,0},{2,1},{3,2},{4,3},{5,4},{6,5},{7,6},{8,7},{9,8},{10,9},{11,1... | collective-permute-start | bytes 393224 | tf_op jit(solution)/shard_map/ppermute | solution.py:29
  16.0 132.5 %reduce-scatter.7.cloned.1.call-start = ((), (), s32[]{:S(2)}) async-start(), calls=%async_computation.3 | async-start | bytes 1880064
  36.6 19.9 %copy-start.2 = (bf16[1024,3456]{1,0:T(8,128)(2,1)}, bf16[1024,3456]{1,0:T(8,128)(2,1)S(1)}, u32[]{:S(2)}) copy-start(bf16[1024,3456]{1,0:T(8,128)(2,1)S(1)} %constant_dynamic-update-slice_fusion.54) | copy-start | bytes 21233668
  69.5 15.0 %collective-permute-start.2 = (bf16[64,4,128]{2,1,0:T(4,128)(2,1)S(1)}, bf16[64,4,128]{2,1,0:T(4,128)(2,1)S(1)}, u32[]{:S(2)}, u32[]{:S(2)}) collective-permute-start(bf16[64,4,128]{2,1,0:T(4,128)(2,1)S(1)} %get-tuple-element.86), channel_id=1, source_target_pairs={{0,1},{1,2},{2,3},{3,4},{4,5},{5,6},{6,7},{7,8},{8,9},{9,10},{10,1... | collective-permute-start | bytes 196616 | tf_op jit(solution)/shard_map/ppermute | solution.py:28
  71.7 12.9 %collective-permute-start.3 = (bf16[64,4,128]{2,1,0:T(4,128)(2,1)S(1)}, bf16[64,4,128]{2,1,0:T(4,128)(2,1)S(1)}, u32[]{:S(2)}, u32[]{:S(2)}) collective-permute-start(bf16[64,4,128]{2,1,0:T(4,128)(2,1)S(1)} %get-tuple-element.87), channel_id=1, source_target_pairs={{1,0},{2,1},{3,2},{4,3},{5,4},{6,5},{7,6},{8,7},{9,8},{10,9},{11,1... | collective-permute-start | bytes 196616 | tf_op jit(solution)/shard_map/ppermute | solution.py:29
  84.5 127.5 %reduce-scatter.9.cloned.1.call-start = ((), (), s32[]{:S(2)}) async-start(), calls=%async_computation.4 | async-start | bytes 1880064
  95.4 6.5 %copy-start.1 = (bf16[3456,256]{1,0:T(8,128)(2,1)S(1)}, bf16[3456,256]{1,0:T(8,128)(2,1)}, u32[]{:S(2)}) copy-start(bf16[3456,256]{1,0:T(8,128)(2,1)} %all-gather.2.cloned.1.call-done) | copy-start | bytes 5308420
  95.6 2.9 %copy-start = (bf16[1024,3456]{1,0:T(8,128)(2,1)}, bf16[1024,3456]{1,0:T(8,128)(2,1)S(1)}, u32[]{:S(2)}) copy-start(bf16[1024,3456]{1,0:T(8,128)(2,1)S(1)} %constant_dynamic-update-slice_fusion.27) | copy-start | bytes 21233668
Sparse Core Ops, SparseCore 0:
  16.1 44.9 all-gather.1
  84.6 63.7 reduce-scatter.6
  152.8 59.1 reduce-scatter.8

commit v2 on v1

--- a/solution.py
+++ b/solution.py
@@ -1,7 +1,11 @@
+import functools
+
 import jax
 import jax.numpy as jnp
 import numpy as np
 from jax import lax
+from jax.experimental import pallas as pl
+from jax.experimental.pallas import tpu as pltpu
 from jax.sharding import PartitionSpec as P
 
 BS = 4
@@ -28,6 +32,119 @@
     before = lax.ppermute(packed[:, rim_count:], "tx", up)
     after = lax.ppermute(packed[:, :rim_count], "tx", down)
     return (before, after)
+
+
+def bit_orders(size):
+    count = size.bit_length() - 1
+    middle = 1 + (count - 1) // 2
+    rest = list(range(middle, count)) + list(range(1, middle))
+    return (list(range(count)), [0] + rest)
+
+
+def halving_kernel(size, orders, first, second, out_first, out_second, *scratch):
+    steps = size.bit_length() - 1
+    sends, recvs, sums = (scratch[: 2 * steps], scratch[2 * steps : 4 * steps], scratch[4 * steps : -2])
+    send_sem, recv_sem = scratch[-2:]
+    me = lax.axis_index("tx")
+    barrier = pltpu.get_barrier_semaphore()
+
+    def bit_of(bit):
+        return me // (1 << bit) % 2
+
+    def partner(bit):
+        return me + (1 - 2 * bit_of(bit)) * (1 << bit)
+
+    for bit in range(steps):
+        pl.semaphore_signal(
+            barrier, inc=1, device_id={"tx": partner(bit)}, device_id_type=pl.DeviceIdType.MESH
+        )
+    pl.semaphore_wait(barrier, steps)
+
+    held = [lambda i: first[i], lambda i: second[i]]
+    left = [list(range(steps)), list(range(steps))]
+    copies = [[], []]
+    outs = (out_first, out_second)
+    for step in range(steps + 1):
+        for stream in range(2):
+            if step:
+                arrived = recvs[stream * steps + step - 1]
+                copies[stream][-1].wait_recv()
+                kept = keep[stream]
+
+                def read(i, kept=kept, arrived=arrived):
+                    return kept(i) + arrived[i].astype(jnp.float32)
+
+            else:
+                read = held[stream]
+                if stream == 0:
+                    keep = [None, None]
+            if step == steps:
+                outs[stream][...] = read(0)
+                continue
+            bit = orders[stream][step]
+            low = 1 << left[stream].index(bit)
+            left[stream].remove(bit)
+            half = size >> (step + 1)
+            mine = bit_of(bit)
+
+            def entry(j, side, low=low):
+                return j // low * (2 * low) + side * low + j % low
+
+            out = sends[stream * steps + step]
+
+            def pack(j, carry, out=out, read=read, entry=entry, mine=mine):
+                out[j] = read(entry(j, 1 - mine)).astype(out.dtype)
+                return carry
+
+            lax.fori_loop(0, half, pack, 0)
+            copy = pltpu.make_async_remote_copy(
+                src_ref=out,
+                dst_ref=recvs[stream * steps + step],
+                send_sem=send_sem.at[stream, step],
+                recv_sem=recv_sem.at[stream, step],
+                device_id={"tx": partner(bit)},
+                device_id_type=pl.DeviceIdType.MESH,
+            )
+            copy.start()
+            copies[stream].append(copy)
+            total = sums[stream * steps + step]
+
+            def fold(j, carry, total=total, read=read, entry=entry, mine=mine):
+                total[j] = read(entry(j, mine))
+                return carry
+
+            lax.fori_loop(0, half, fold, 0)
+            keep[stream] = lambda i, total=total: total[i]
+    for stream in range(2):
+        for copy in copies[stream]:
+            copy.wait_send()
+
+
+def reduce_both(first, second):
+    size = lax.axis_size("tx")
+    steps = size.bit_length() - 1
+    rows = first.shape[0] // size
+    tall = -(-rows // 16) * 16
+    lanes = first.shape[1]
+    first, second = (
+        jnp.pad(x.reshape(size, rows, lanes), ((0, 0), (0, tall - rows), (0, 0)))
+        for x in (first, second)
+    )
+    halves = [(size >> (step + 1), tall, lanes) for step in range(steps)] * 2
+    whole = pl.BlockSpec(memory_space=pltpu.VMEM)
+    outs = pl.pallas_call(
+        functools.partial(halving_kernel, size, bit_orders(size)),
+        out_shape=[jax.ShapeDtypeStruct((tall, lanes), jnp.float32)] * 2,
+        in_specs=[whole] * 2,
+        out_specs=[whole] * 2,
+        scratch_shapes=[pltpu.VMEM(shape, jnp.bfloat16) for shape in halves * 2]
+        + [pltpu.VMEM(shape, jnp.float32) for shape in halves]
+        + [pltpu.SemaphoreType.DMA((2, steps)), pltpu.SemaphoreType.DMA((2, steps))],
+        compiler_params=pltpu.CompilerParams(
+            collective_id=0, has_side_effects=True, vmem_limit_bytes=32 * 1024 * 1024
+        ),
+    )(first, second)
+    return [x[:rows] for x in outs]
 
 
 def on_device(features, nbr_table, rim_slots, w_first, w_second, cotangent):
@@ -94,7 +211,6 @@
     grad_mid = (back * sigmoid_mid * (1.0 + first_sum * (1.0 - sigmoid_mid))).astype(jnp.bfloat16)
     contract = (((0,), (0,)), ((), ()))
     term_first = lax.dot_general(inputs, grad_mid, contract, preferred_element_type=jnp.float32)
-    grad_first = lax.psum_scatter(term_first, "tx", scatter_dimension=0, tiled=True)
 
     middle = windows(halo(hidden.reshape(vox_count, SLOTS, channels)))
     out_map = jnp.dot(middle, full_second, preferred_element_type=jnp.float32).astype(jnp.bfloat16)
@@ -103,7 +219,7 @@
         stacked[..., channels:], ((0, 0), (0, SLOTS - capacity), (0, 0))
     ).reshape(-1, channels)
     term_second = lax.dot_general(middle, cot_rows, contract, preferred_element_type=jnp.float32)
-    grad_second = lax.psum_scatter(term_second, "tx", scatter_dimension=0, tiled=True)
+    grad_first, grad_second = reduce_both(term_first, term_second)
     return (out_map, grad_first, grad_second)
 
 

time: 219 us -> 167 us (0.76)
  waiting for transfers between devices: 108 us -> 3.74 us
  local copies, waits for them, and re-layouts: 57.9 us -> 84.3 us
  Pallas kernels: 0 us -> 25 us
    unnamed x5 -> x1, waiting for transfers between devices: 104 us -> 0.02 us
    pallas_call x0 -> x1, Pallas kernels: none -> 25 us  [reduce_both(): pl.pallas_call(functools.partial(halving_kernel, size, bit_orders(size)),...]
    unnamed x88 -> x85, local copies, waits for them, and re-layouts: 30.5 us -> 43.5 us
    dot_general x0 -> x1, local copies, waits for them, and re-layouts: none -> 10.2 us  [on_device(): lax.dot_general(middle, cot_rows, contract, preferred_element_type=jnp.fl...]
  transfers between devices with their start and end apart: 7 -> 5, of which waited for: 3 -> 1; matrix products, arithmetic and copies ran while one was open for 34% -> 32% of each run, Pallas kernels for 0% -> 0%
where the time goes in v2:
time: 167 us; the launch traced here: 166 us
  local copies, waits for them, and re-layouts  84.3 us (50%)
  matrix products  25.4 us (15%)
  Pallas kernels  25 us (15%)
  between operations  14.6 us (9%)
  starting transfers between devices  7.33 us (4%)
  other arithmetic  6.15 us (4%)
  waiting for transfers between devices  3.74 us (2%)
    unnamed x85, local copies, waits for them, and re-layouts  43.5 us
    pallas_call x1, Pallas kernels, reduce_both(): pl.pallas_call(functools.partial(halving_kernel, size, bit_orders(size)),...  25 us
    gather x2, local copies, waits for them, and re-layouts, halo(): jnp.take(extended.reshape(-1, blocks.shape[2]), index, axis=0, mode='clip')  17.8 us
    dot_general x1, local copies, waits for them, and re-layouts, on_device(): lax.dot_general(middle, cot_rows, contract, preferred_element_type=jnp.fl...  10.2 us
    dot_general x1, matrix products, on_device(): first_sum = jnp.dot(inputs, full_first, preferred_element_type=jnp.float32)  5.19 us
    slice x5, local copies, waits for them, and re-layouts, windows(): part = padded[a:a + BS, b:b + BS, c:c + BS]  5.07 us
    dot_general x1, matrix products, on_device(): lax.dot_general(inputs, grad_mid, contract, preferred_element_type=jnp.fl...  5.07 us
    dot_general x1, matrix products, on_device(): lax.dot_general(middle, cot_rows, contract, preferred_element_type=jnp.fl...  5.07 us
  transfers between devices with their start and end apart: 5, of which 1 were waited for; matrix products, arithmetic and copies ran while one was open for 32% of the time, Pallas kernels for 0%

profile of v2, /device:TPU:0, one launch (start us, length us, event | category | flops | bytes accessed | tf_op | source)
XLA Modules:
  0.0 166.4 jit_solution(10416726942402810487)
XLA Ops:
  7.2 1.1 maximum_bitcast_fusion
  9.9 2.4 %collective-permute-start = (bf16[64,4,256]{2,1,0:T(4,128)(2,1)S(1)}, bf16[64,4,256]{2,1,0:T(4,128)(2,1)S(1)}, u32[]{:S(2)}, u32[]{:S(2)}) collective-permute-start(bf16[64,4,256]{2,1,0:T(4,128)(2,1)S(1)} %get-tuple-element.88), channel_id=1, source_target_pairs={{0,1},{1,2},{2,3},{3,4},{4,5},{5,6},{6,7},{7,8},{8,9},{9,10},{10,1... | collective-permute-start | bytes 393224 | tf_op jit(solution)/shard_map/ppermute | solution.py:32
  12.3 1.3 collective-permute-start.1
  13.6 1.5 pad_maximum_fusion
  15.1 0.8 copy.60
  17.3 0.8 broadcast_add_fusion
  19.1 10.6 %gather_fusion.1 = bf16[3456,256]{1,0:T(8,128)(2,1)S(1)} fusion(bf16[1536,256]{1,0:T(8,128)(2,1)S(1)} %bitcast.115, s32[4096]{0:T(1024)S(1)} %pad_clamp_fusion), kind=kCustom, calls=%fused_computation.1 | custom fusion | bytes 3552768 | tf_op jit(solution)/shard_map/jit(_take)/gather | solution.py:182
  29.8 1.3 fusion.6
  31.1 1.3 fusion.5
  32.4 0.9 fusion.7
  35.9 0.8 constant_dynamic-update-slice_fusion.25
  36.7 1.2 constant_dynamic-update-slice_fusion.24
  37.9 1.1 constant_dynamic-update-slice_fusion.23
  39.7 0.8 constant_dynamic-update-slice_fusion.21
  40.5 0.8 constant_dynamic-update-slice_fusion.20
  41.3 0.8 constant_dynamic-update-slice_fusion.19
  43.5 0.8 constant_dynamic-update-slice_fusion.16
  44.3 0.8 constant_dynamic-update-slice_fusion.15
  45.1 0.8 constant_dynamic-update-slice_fusion.14
  45.8 0.8 constant_dynamic-update-slice_fusion.13
  46.6 0.8 constant_dynamic-update-slice_fusion.12
  47.4 0.8 constant_dynamic-update-slice_fusion.11
  48.2 0.8 constant_dynamic-update-slice_fusion.10
  49.0 0.7 constant_dynamic-update-slice_fusion.9
  49.7 0.8 constant_dynamic-update-slice_fusion.8
  50.5 0.7 constant_dynamic-update-slice_fusion.7
  51.2 0.8 constant_dynamic-update-slice_fusion.6
  52.7 0.8 constant_dynamic-update-slice_fusion.4
  53.5 0.8 constant_dynamic-update-slice_fusion.3
  55.0 0.8 constant_dynamic-update-slice_fusion.1
  56.5 3.7 %all-gather.2.cloned.1.call-done = bf16[3456,256]{1,0:T(8,128)(2,1)} async-done(((bf16[216,256]{1,0:T(8,128)(2,1)}), bf16[3456,256]{1,0:T(8,128)(2,1)}) %all-gather.2.cloned.1.call-update) | async-done | bytes 1769488 | tf_op jit(solution)/shard_map/all_gather | solution.py:158
  60.2 1.2 slice.490
  61.5 1.3 copy.62
  62.8 5.2 %multiply_convert_fusion = (bf16[1024,128]{1,0:T(8,128)(2,1)S(1)}, f32[1024,128]{1,0:T(8,128)S(1)}) fusion(bf16[1024,3456]{1,0:T(8,128)(2,1)} %constant_dynamic-update-slice_fusion, bf16[3456,256]{1,0:T(8,128)(2,1)} %all-gather.2.cloned.1.call-done), kind=kOutput, calls=%fused_computation.13 | convolution fusion | flops 906625024 | bytes 8749056 | tf_op jit(solution)/shard_map/dot_general | solution.py:207
  68.6 2.2 %collective-permute-start.2 = (bf16[64,4,128]{2,1,0:T(4,128)(2,1)S(1)}, bf16[64,4,128]{2,1,0:T(4,128)(2,1)S(1)}, u32[]{:S(2)}, u32[]{:S(2)}) collective-permute-start(bf16[64,4,128]{2,1,0:T(4,128)(2,1)S(1)} %get-tuple-element.90), channel_id=1, source_target_pairs={{0,1},{1,2},{2,3},{3,4},{4,5},{5,6},{6,7},{7,8},{8,9},{9,10},{10,1... | collective-permute-start | bytes 196616 | tf_op jit(solution)/shard_map/ppermute | solution.py:32
  70.8 1.5 collective-permute-start.3
  72.3 5.0 %fusion.1 = bf16[1024,128]{1,0:T(8,128)(2,1)S(1)} fusion(bf16[1024,3456]{1,0:T(8,128)(2,1)} %copy-done.1, bf16[3456,128]{1,0:T(8,128)(2,1)S(1)} %bitcast.209, f32[1024,128]{1,0:T(8,128)S(1)} %get-tuple-element.93), kind=kOutput, calls=%fused_computation.7 | convolution fusion | flops 907149312 | bytes 8749056 | tf_op jit(solution)/shard_map/dot_general | solution.py:210
  77.3 5.1 %fusion.12 = f32[3456,128]{1,0:T(8,128)S(1)} fusion(bf16[1024,3456]{1,0:T(8,128)(2,1)} %constant_dynamic-update-slice_fusion, bf16[1024,128]{1,0:T(8,128)(2,1)S(1)} %fusion.1), kind=kOutput, calls=%fused_computation.113 | convolution fusion | flops 905969664 | bytes 9109504 | tf_op jit(solution)/shard_map/dot_general | solution.py:213
  82.8 7.1 %gather_fusion.2 = bf16[3456,128]{1,0:T(8,128)(2,1)S(1)} fusion(bf16[1536,128]{1,0:T(8,128)(2,1)S(1)} %bitcast.119, s32[4096]{0:T(1024)S(1)} %pad_clamp_fusion), kind=kCustom, calls=%fused_computation.2 | custom fusion | bytes 1783296 | tf_op jit(solution)/shard_map/jit(_take)/gather | solution.py:182
  90.3 1.3 fusion.8
  91.6 0.8 constant_dynamic-update-slice_fusion.53
  94.7 0.7 constant_dynamic-update-slice_fusion.49
  95.4 0.8 constant_dynamic-update-slice_fusion.48
  96.2 0.8 constant_dynamic-update-slice_fusion.47
  96.9 0.8 constant_dynamic-update-slice_fusion.46
  97.7 0.8 constant_dynamic-update-slice_fusion.45
  99.2 0.8 constant_dynamic-update-slice_fusion.43
  100.0 0.8 constant_dynamic-update-slice_fusion.42
  100.7 0.8 constant_dynamic-update-slice_fusion.41
  101.5 0.7 constant_dynamic-update-slice_fusion.40
  102.2 0.8 constant_dynamic-update-slice_fusion.39
  104.5 0.8 constant_dynamic-update-slice_fusion.36
  105.2 0.8 constant_dynamic-update-slice_fusion.35
  106.0 0.7 constant_dynamic-update-slice_fusion.34
  106.7 0.7 constant_dynamic-update-slice_fusion.33
  108.2 0.8 constant_dynamic-update-slice_fusion.31
  109.0 0.8 constant_dynamic-update-slice_fusion.30
  109.7 0.7 constant_dynamic-update-slice_fusion.29
  110.5 0.8 constant_dynamic-update-slice_fusion.28
  111.2 0.8 constant_dynamic-update-slice_fusion.27
  112.1 10.2 %copy.63 = bf16[3456,1024]{1,0:T(8,128)(2,1)} copy(bf16[3456,1024]{0,1:T(8,128)(2,1)} %bitcast.95) | data formatting | bytes 14155776 | tf_op jit(solution)/shard_map/dot_general | solution.py:221
  122.3 5.1 %fusion.13 = f32[16,216,128]{2,1,0:T(8,128)S(1)} fusion(bf16[16,216,1024]{2,1,0:T(8,128)(2,1)} %bitcast.122, bf16[1024,128,1]{1,0,2:T(8,128)(2,1)S(1)} %bitcast.125), kind=kOutput, calls=%fused_computation.114 | convolution fusion | flops 905969664 | bytes 9109504 | tf_op jit(solution)/shard_map/dot_general | solution.py:221
  127.5 25.0 %shard_map.103 = (f32[224,128]{1,0:T(8,128)S(1)}, f32[224,128]{1,0:T(8,128)S(1)}) custom-call(f32[16,224,128]{2,1,0:T(8,128)S(1)} %pad.16.first, f32[16,224,128]{2,1,0:T(8,128)S(1)} %pad.18.second), custom_call_target="tpu_custom_call" | custom-call | tf_op jit(solution)/shard_map/pallas_call | solution.py:135
  153.8 5.0 %convolution_convert_fusion = bf16[1024,128]{1,0:T(8,128)(2,1)S(1)} fusion(bf16[1024,3456]{1,0:T(8,128)(2,1)} %constant_dynamic-update-slice_fusion.27, bf16[3456,256]{1,0:T(8,128)(2,1)S(1)} %copy-done), kind=kOutput, calls=%fused_computation.8 | convolution fusion | flops 906100736 | bytes 8224768 | tf_op jit(solution)/shard_map/dot_general | solution.py:216
  (79 shorter events, 19.7 us)
Async XLA Ops:
  7.2 53.0 %all-gather.2.cloned.1.call-start = ((), (), s32[]{:S(2)}) async-start(), calls=%async_computation | async-start | bytes 1880064 | tf_op jit(solution)/shard_map/all_gather | solution.py:158
  9.9 8.6 %collective-permute-start = (bf16[64,4,256]{2,1,0:T(4,128)(2,1)S(1)}, bf16[64,4,256]{2,1,0:T(4,128)(2,1)S(1)}, u32[]{:S(2)}, u32[]{:S(2)}) collective-permute-start(bf16[64,4,256]{2,1,0:T(4,128)(2,1)S(1)} %get-tuple-element.88), channel_id=1, source_target_pairs={{0,1},{1,2},{2,3},{3,4},{4,5},{5,6},{6,7},{7,8},{8,9},{9,10},{10,1... | collective-permute-start | bytes 393224 | tf_op jit(solution)/shard_map/ppermute | solution.py:32
  12.3 6.3 %collective-permute-start.1 = (bf16[64,4,256]{2,1,0:T(4,128)(2,1)S(1)}, bf16[64,4,256]{2,1,0:T(4,128)(2,1)S(1)}, u32[]{:S(2)}, u32[]{:S(2)}) collective-permute-start(bf16[64,4,256]{2,1,0:T(4,128)(2,1)S(1)} %get-tuple-element.89), channel_id=1, source_target_pairs={{1,0},{2,1},{3,2},{4,3},{5,4},{6,5},{7,6},{8,7},{9,8},{10,9},{11,1... | collective-permute-start | bytes 393224 | tf_op jit(solution)/shard_map/ppermute | solution.py:33
  35.9 19.9 %copy-start.1 = (bf16[1024,3456]{1,0:T(8,128)(2,1)}, bf16[1024,3456]{1,0:T(8,128)(2,1)S(1)}, u32[]{:S(2)}) copy-start(bf16[1024,3456]{1,0:T(8,128)(2,1)S(1)} %constant_dynamic-update-slice_fusion.54) | copy-start | bytes 21233668
  68.6 14.0 %collective-permute-start.2 = (bf16[64,4,128]{2,1,0:T(4,128)(2,1)S(1)}, bf16[64,4,128]{2,1,0:T(4,128)(2,1)S(1)}, u32[]{:S(2)}, u32[]{:S(2)}) collective-permute-start(bf16[64,4,128]{2,1,0:T(4,128)(2,1)S(1)} %get-tuple-element.90), channel_id=1, source_target_pairs={{0,1},{1,2},{2,3},{3,4},{4,5},{5,6},{6,7},{7,8},{8,9},{9,10},{10,1... | collective-permute-start | bytes 196616 | tf_op jit(solution)/shard_map/ppermute | solution.py:32
  70.8 11.8 %collective-permute-start.3 = (bf16[64,4,128]{2,1,0:T(4,128)(2,1)S(1)}, bf16[64,4,128]{2,1,0:T(4,128)(2,1)S(1)}, u32[]{:S(2)}, u32[]{:S(2)}) collective-permute-start(bf16[64,4,128]{2,1,0:T(4,128)(2,1)S(1)} %get-tuple-element.91), channel_id=1, source_target_pairs={{1,0},{2,1},{3,2},{4,3},{5,4},{6,5},{7,6},{8,7},{9,8},{10,9},{11,1... | collective-permute-start | bytes 196616 | tf_op jit(solution)/shard_map/ppermute | solution.py:33
  127.4 26.5 %copy-start = (bf16[3456,256]{1,0:T(8,128)(2,1)S(1)}, bf16[3456,256]{1,0:T(8,128)(2,1)}, u32[]{:S(2)}) copy-start(bf16[3456,256]{1,0:T(8,128)(2,1)} %all-gather.2.cloned.1.call-done) | copy-start | bytes 5308420
Sparse Core Ops, SparseCore 0:
  15.2 44.9 all-gather.1

commit v3 on v2

--- a/solution.py
+++ b/solution.py
@@ -147,6 +147,96 @@
     return [x[:rows] for x in outs]
 
 
+CONTRACT = (((0,), (0,)), ((), ()))
+
+
+def fill_windows(win, padded):
+    channels = padded.shape[-1]
+    for offset in range(27):
+        a, b, c = (offset // 9, offset // 3 % 3, offset % 3)
+        for i in range(BS):
+            part = padded[a + i, b : b + BS, c : c + BS]
+            rows = BS * BS * SLOTS
+            win[i * rows : (i + 1) * rows, offset * channels : (offset + 1) * channels] = (
+                part.reshape(rows, channels)
+            )
+
+
+def row_tiles(win, body):
+    rows = BS * BS * SLOTS
+
+    def step(i, carry):
+        body(pl.ds(pl.multiple_of(i * rows, rows), rows))
+        return carry
+
+    lax.fori_loop(0, win.shape[0] // rows, step, 0)
+
+
+def kernel_gradient(win, cots, term):
+    channels = term.shape[1]
+    wide = 3 * channels
+
+    def step(i, carry):
+        columns = pl.ds(pl.multiple_of(i * wide, wide), wide)
+        term[columns, :] = lax.dot_general(
+            win[:, columns], cots[...], CONTRACT, preferred_element_type=jnp.float32
+        )
+        return carry
+
+    lax.fori_loop(0, win.shape[1] // wide, step, 0)
+
+
+def first_kernel(feats, cots, w_first, flipped, hidden, term, win, back, grad_mid):
+    fill_windows(win, cots)
+
+    def backward(rows):
+        back[rows, :] = jnp.dot(win[rows, :], flipped[...], preferred_element_type=jnp.float32)
+
+    row_tiles(win, backward)
+    fill_windows(win, feats)
+
+    def forward(rows):
+        first_sum = jnp.dot(win[rows, :], w_first[...], preferred_element_type=jnp.float32)
+        gate = jax.nn.sigmoid(first_sum)
+        hidden[rows, :] = (first_sum * gate).astype(hidden.dtype)
+        grad_mid[rows, :] = (
+            back[rows, :] * gate * (1.0 + first_sum * (1.0 - gate))
+        ).astype(grad_mid.dtype)
+
+    row_tiles(win, forward)
+    kernel_gradient(win, grad_mid, term)
+
+
+def second_kernel(mids, cots, w_second, out_map, term, win):
+    fill_windows(win, mids)
+
+    def forward(rows):
+        out_map[rows, :] = jnp.dot(
+            win[rows, :], w_second[...], preferred_element_type=jnp.float32
+        ).astype(out_map.dtype)
+
+    row_tiles(win, forward)
+    kernel_gradient(win, cots, term)
+
+
+def local_call(body, operands, extra):
+    depth, channels = operands[2].shape
+    rows = BS**3 * SLOTS
+    whole = pl.BlockSpec(memory_space=pltpu.VMEM)
+    return pl.pallas_call(
+        body,
+        out_shape=[
+            jax.ShapeDtypeStruct((rows, channels), jnp.bfloat16),
+            jax.ShapeDtypeStruct((depth, channels), jnp.float32),
+        ],
+        in_specs=[whole] * len(operands),
+        out_specs=[whole] * 2,
+        scratch_shapes=[pltpu.VMEM((rows, depth), jnp.bfloat16)]
+        + [pltpu.VMEM((rows, channels), kind) for kind in extra],
+        compiler_params=pltpu.CompilerParams(vmem_limit_bytes=40 * 1024 * 1024),
+    )(*operands)
+
+
 def on_device(features, nbr_table, rim_slots, w_first, w_second, cotangent):
     capacity, vox_count, channels = features.shape
     rim_count = rim_slots.shape[1] // 2
@@ -155,9 +245,10 @@
     width = zero_slot + 4
     brick, local = halo_tables(BS)
 
-    both_w = lax.all_gather(
-        jnp.concatenate([w_first, w_second], axis=1), "tx", axis=0, tiled=True
-    )
+    own_w, features, cotangent = lax.optimization_barrier(
+        (jnp.concatenate([w_first, w_second], axis=1), features, cotangent)
+    )
+    both_w = lax.all_gather(own_w, "tx", axis=0, tiled=True)
 
     table = jnp.pad(
         nbr_table, ((0, SLOTS - capacity), (0, 0)), constant_values=zero_slot
@@ -185,18 +276,8 @@
         wide = BS + 2
         return picked.reshape(wide, wide, wide, SLOTS, blocks.shape[2])
 
-    def windows(padded):
-        parts = []
-        for offset in range(27):
-            a, b, c = (offset // 9, offset // 3 % 3, offset % 3)
-            part = padded[a : a + BS, b : b + BS, c : c + BS]
-            parts.append(part.reshape(vox_count * SLOTS, channels))
-        return jnp.concatenate(parts, axis=1)
-
     stacked = jnp.concatenate([features, cotangent], axis=2).transpose(1, 0, 2)
     outer = halo(stacked)
-    inputs = windows(outer[..., :channels])
-    cots = windows(outer[..., channels:])
     full_first, full_second = (both_w[:, :channels], both_w[:, channels:])
     kernel_count = full_second.shape[0] // channels
     flipped = (
@@ -204,21 +285,17 @@
         .transpose(0, 2, 1)
         .reshape(-1, channels)
     )
-    first_sum = jnp.dot(inputs, full_first, preferred_element_type=jnp.float32)
-    sigmoid_mid = jax.nn.sigmoid(first_sum)
-    hidden = (first_sum * sigmoid_mid).astype(jnp.bfloat16)
-    back = jnp.dot(cots, flipped, preferred_element_type=jnp.float32)
-    grad_mid = (back * sigmoid_mid * (1.0 + first_sum * (1.0 - sigmoid_mid))).astype(jnp.bfloat16)
-    contract = (((0,), (0,)), ((), ()))
-    term_first = lax.dot_general(inputs, grad_mid, contract, preferred_element_type=jnp.float32)
-
-    middle = windows(halo(hidden.reshape(vox_count, SLOTS, channels)))
-    out_map = jnp.dot(middle, full_second, preferred_element_type=jnp.float32).astype(jnp.bfloat16)
-    out_map = out_map.reshape(vox_count, SLOTS, channels)[:, :capacity].transpose(1, 0, 2)
+    hidden, term_first = local_call(
+        first_kernel,
+        (outer[..., :channels], outer[..., channels:], full_first, flipped),
+        (jnp.float32, jnp.bfloat16),
+    )
     cot_rows = jnp.pad(
         stacked[..., channels:], ((0, 0), (0, SLOTS - capacity), (0, 0))
     ).reshape(-1, channels)
-    term_second = lax.dot_general(middle, cot_rows, contract, preferred_element_type=jnp.float32)
+    middle = halo(hidden.reshape(vox_count, SLOTS, channels))
+    out_map, term_second = local_call(second_kernel, (middle, cot_rows, full_second), ())
+    out_map = out_map.reshape(vox_count, SLOTS, channels)[:, :capacity].transpose(1, 0, 2)
     grad_first, grad_second = reduce_both(term_first, term_second)
     return (out_map, grad_first, grad_second)
 

time: 167 us -> 125 us (0.75)
  local copies, waits for them, and re-layouts: 84.3 us -> 32.3 us
  matrix products: 25.4 us -> 0 us
  waiting for transfers between devices: 3.74 us -> 26.4 us
  Pallas kernels: 25 us -> 40.7 us
  other arithmetic: 6.15 us -> 4.14 us
    unnamed x85 -> x25, local copies, waits for them, and re-layouts: 43.5 us -> 3.35 us
    dot_general x5 -> x0, matrix products: 25.4 us -> none  [the longest x1 5.19 us: on_device(): first_sum = jnp.dot(inputs, full_first, preferred_element_type=jnp.float32)]
    all_gather x1, waiting for transfers between devices: 3.72 us -> 22.1 us  [on_device(): both_w = lax.all_gather(own_w, 'tx', axis=0, tiled=True)]
    pallas_call x0 -> x2, Pallas kernels: none -> 18 us  [local_call(): pl.pallas_call(body, out_shape=[jax.ShapeDtypeStruct((rows, channels), jn...]
    dot_general x1 -> x0, local copies, waits for them, and re-layouts: 10.2 us -> none  [on_device(): lax.dot_general(middle, cot_rows, contract, preferred_element_type=jnp.fl...]
    ppermute x2, waiting for transfers between devices: 0.01 us -> 4.32 us  [neighbours(): after = lax.ppermute(packed[:, :rim_count], 'tx', down)]
    slice x5 -> x1, local copies, waits for them, and re-layouts: 5.07 us -> 1.75 us  [on_device(): outer[..., channels:]]
    pallas_call x1, Pallas kernels: 25 us -> 22.7 us  [reduce_both(): pl.pallas_call(functools.partial(halving_kernel, size, bit_orders(size)),...]
  transfers between devices with their start and end apart: 5 -> 5, of which waited for: 1 -> 3; matrix products, arithmetic and copies ran while one was open for 32% -> 13% of each run, Pallas kernels for 0% -> 0%
where the time goes in v3:
time: 125 us
  Pallas kernels  40.7 us (33%)
  local copies, waits for them, and re-layouts  32.3 us (26%)
  waiting for transfers between devices  26.4 us (21%)
  between operations  14.4 us (12%)
  starting transfers between devices  7.16 us (6%)
  other arithmetic  4.14 us (3%)
    pallas_call x1, Pallas kernels, reduce_both(): pl.pallas_call(functools.partial(halving_kernel, size, bit_orders(size)),...  22.7 us
    all_gather x1, waiting for transfers between devices, on_device(): both_w = lax.all_gather(own_w, 'tx', axis=0, tiled=True)  22.1 us
    gather x2, local copies, waits for them, and re-layouts, halo(): jnp.take(extended.reshape(-1, blocks.shape[2]), index, axis=0, mode='clip')  19 us
    pallas_call x2, Pallas kernels, local_call(): pl.pallas_call(body, out_shape=[jax.ShapeDtypeStruct((rows, channels), jn...  18 us
    ppermute x2, starting transfers between devices, neighbours(): before = lax.ppermute(packed[:, rim_count:], 'tx', up)  4.54 us
    ppermute x2, waiting for transfers between devices, neighbours(): after = lax.ppermute(packed[:, :rim_count], 'tx', down)  4.32 us
    unnamed x25, local copies, waits for them, and re-layouts  3.35 us
    transpose x2, local copies, waits for them, and re-layouts, on_device(): flipped = full_second.reshape(kernel_count, channels, channels)[::-1].tra...  3.18 us
  transfers between devices with their start and end apart: 5, of which 3 were waited for; matrix products, arithmetic and copies ran while one was open for 13% of the time, Pallas kernels for 0%

profile of v3, /device:TPU:0, one launch (start us, length us, event | category | flops | bytes accessed | tf_op | source)
XLA Modules:
  0.0 125.0 jit_solution(9219277173096801860)
XLA Ops:
  7.2 0.0 copy-start.9
  7.2 0.0 copy-start.10
  7.2 0.0 copy-start.5
  7.2 0.0 all-gather.2.cloned.1.call-start
  7.2 1.5 %pad_maximum_fusion = bf16[216,256]{1,0:T(8,128)(2,1)} fusion(bf16[216,128]{1,0:T(8,128)(2,1)} %param.12, bf16[216,128]{1,0:T(8,128)(2,1)} %param.11), kind=kLoop, calls=%fused_computation.10 | loop fusion | flops 221184 | bytes 221184 | tf_op jit(solution)/shard_map/concatenate | solution.py:249
  8.7 0.0 all-gather.2.cloned.1.call-update
  8.8 1.1 maximum_bitcast_fusion
  9.8 0.0 copy-start.2
  9.9 0.0 copy-start.8
  9.9 0.2 copy.23
  10.1 0.0 copy-done.10
  10.1 0.0 copy-start.3
  10.1 0.6 select_reduce_fusion
  10.8 0.1 fusion.2
  10.8 2.4 %collective-permute-start = (bf16[64,4,256]{2,1,0:T(4,128)(2,1)S(1)}, bf16[64,4,256]{2,1,0:T(4,128)(2,1)S(1)}, u32[]{:S(2)}, u32[]{:S(2)}) collective-permute-start(bf16[64,4,256]{2,1,0:T(4,128)(2,1)S(1)} %get-tuple-element.25), channel_id=1, source_target_pairs={{0,1},{1,2},{2,3},{3,4},{4,5},{5,6},{6,7},{7,8},{8,9},{9,10},{10,1... | collective-permute-start | bytes 393224 | tf_op jit(solution)/shard_map/ppermute | solution.py:32
  13.2 0.0 copy-done.3
  13.2 1.3 %collective-permute-start.1 = (bf16[64,4,256]{2,1,0:T(4,128)(2,1)S(1)}, bf16[64,4,256]{2,1,0:T(4,128)(2,1)S(1)}, u32[]{:S(2)}, u32[]{:S(2)}) collective-permute-start(bf16[64,4,256]{2,1,0:T(4,128)(2,1)S(1)} %get-tuple-element.26), channel_id=1, source_target_pairs={{1,0},{2,1},{3,2},{4,3},{5,4},{6,5},{7,6},{8,7},{9,8},{10,9},{11,1... | collective-permute-start | bytes 393224 | tf_op jit(solution)/shard_map/ppermute | solution.py:33
  14.5 0.0 copy-done.5
  14.5 0.1 copy.27
  14.6 0.0 copy-done.9
  14.7 0.7 gather_fusion
  15.4 0.0 copy-done.8
  15.4 0.1 broadcast_add_fusion
  15.5 0.1 reshape.128
  15.6 0.1 pad.26.clone
  15.7 0.0 copy-start.6
  15.7 0.0 collective-permute-done
  15.7 2.9 %collective-permute-done.1 = bf16[64,4,256]{2,1,0:T(4,128)(2,1)S(1)} collective-permute-done((bf16[64,4,256]{2,1,0:T(4,128)(2,1)S(1)}, bf16[64,4,256]{2,1,0:T(4,128)(2,1)S(1)}, u32[]{:S(2)}, u32[]{:S(2)}) %collective-permute-start.1) | collective-permute-done | bytes 131104 | tf_op jit(solution)/shard_map/ppermute | solution.py:33
  18.6 0.0 copy-done.2
  18.6 0.0 copy-done.6
  18.6 0.1 maximum_maximum_fusion
  18.8 0.4 copy.26
  19.2 10.9 %gather_fusion.1 = bf16[3456,256]{1,0:T(8,128)(2,1)} fusion(bf16[1536,256]{1,0:T(8,128)(2,1)S(1)} %bitcast.32, s32[4096]{0:T(1024)S(1)} %pad_clamp_fusion), kind=kCustom, calls=%fused_computation.1 | custom fusion | bytes 3552768 | tf_op jit(solution)/shard_map/jit(_take)/gather | solution.py:273
  30.2 1.8 %fusion.1 = (bf16[6,6,6,16,128]{4,3,2,1,0:T(8,128)(2,1)S(1)}, bf16[6,6,6,16,128]{4,3,2,1,0:T(8,128)(2,1)S(1)}) fusion(bf16[6,6,6,16,256]{4,3,2,1,0:T(8,128)(2,1)} %bitcast.34), kind=kLoop, calls=%fused_computation.17 | loop fusion | bytes 3538944 | tf_op jit(solution)/shard_map/slice | solution.py:290
  31.9 22.1 %all-gather.2.cloned.1.call-done = bf16[3456,256]{1,0:T(8,128)(2,1)} async-done(((bf16[216,256]{1,0:T(8,128)(2,1)}), bf16[3456,256]{1,0:T(8,128)(2,1)}) %all-gather.2.cloned.1.call-update) | async-done | bytes 1769488 | tf_op jit(solution)/shard_map/all_gather | solution.py:251
  54.0 1.5 %fusion = (bf16[3456,128]{1,0:T(8,128)(2,1)S(1)}, bf16[3456,128]{1,0:T(8,128)(2,1)S(1)}) fusion(bf16[3456,256]{1,0:T(8,128)(2,1)} %all-gather.2.cloned.1.call-done), kind=kLoop, calls=%fused_computation.16 | loop fusion | bytes 3538944 | tf_op jit(solution)/shard_map/slice | solution.py:281
  55.5 1.0 reverse_bitcast_fusion
  56.5 2.2 %copy.28 = bf16[27,128,128]{2,1,0:T(8,128)(2,1)} copy(bf16[27,128,128]{1,2,0:T(8,128)(2,1)} %reverse_bitcast_fusion) | data formatting | bytes 1769472 | tf_op jit(solution)/shard_map/transpose | solution.py:285
  58.7 0.0 copy-start
  58.7 1.2 copy-done
  59.9 0.0 slice-start
  59.9 10.7 %shard_map.103 = (bf16[1024,128]{1,0:T(8,128)(2,1)S(1)}, f32[3456,128]{1,0:T(8,128)S(1)}) custom-call(bf16[6,6,6,16,128]{4,3,2,1,0:T(8,128)(2,1)S(1)} %get-tuple-element.24.feats, bf16[6,6,6,16,128]{4,3,2,1,0:T(8,128)(2,1)S(1)} %get-tuple-element.23.cots, bf16[3456,128]{1,0:T(8,128)(2,1)S(1)} %get-tuple-element.22.w_first, bf16[3456,128]{1,0:T(8,128)(2,1)S(1)} %bitcast.24), custom_call_target="tpu_custom_call" | custom-call | tf_op jit(solution)/shard_map/pallas_call | solution.py:226
  70.6 0.0 copy-done.4
  70.6 0.5 select_reduce_fusion.1
  71.2 2.2 %collective-permute-start.2 = (bf16[64,4,128]{2,1,0:T(4,128)(2,1)S(1)}, bf16[64,4,128]{2,1,0:T(4,128)(2,1)S(1)}, u32[]{:S(2)}, u32[]{:S(2)}) collective-permute-start(bf16[64,4,128]{2,1,0:T(4,128)(2,1)S(1)} %get-tuple-element.27), channel_id=1, source_target_pairs={{0,1},{1,2},{2,3},{3,4},{4,5},{5,6},{6,7},{7,8},{8,9},{9,10},{10,1... | collective-permute-start | bytes 196616 | tf_op jit(solution)/shard_map/ppermute | solution.py:32
  73.4 1.3 %collective-permute-start.3 = (bf16[64,4,128]{2,1,0:T(4,128)(2,1)S(1)}, bf16[64,4,128]{2,1,0:T(4,128)(2,1)S(1)}, u32[]{:S(2)}, u32[]{:S(2)}) collective-permute-start(bf16[64,4,128]{2,1,0:T(4,128)(2,1)S(1)} %get-tuple-element.28), channel_id=1, source_target_pairs={{1,0},{2,1},{3,2},{4,3},{5,4},{6,5},{7,6},{8,7},{9,8},{10,9},{11,1... | collective-permute-start | bytes 196616 | tf_op jit(solution)/shard_map/ppermute | solution.py:33
  74.7 0.0 slice-done
  74.7 0.1 copy.32
  74.8 0.1 pad.16.clone
  74.9 0.0 copy-start.7
  74.9 0.2 pad.17.first
  75.1 0.0 collective-permute-done.2
  75.1 1.4 %collective-permute-done.3 = bf16[64,4,128]{2,1,0:T(4,128)(2,1)S(1)} collective-permute-done((bf16[64,4,128]{2,1,0:T(4,128)(2,1)S(1)}, bf16[64,4,128]{2,1,0:T(4,128)(2,1)S(1)}, u32[]{:S(2)}, u32[]{:S(2)}) %collective-permute-start.3) | collective-permute-done | bytes 65568 | tf_op jit(solution)/shard_map/ppermute | solution.py:33
  76.5 0.0 copy-done.7
  76.5 0.2 maximum_maximum_fusion.1
  76.7 8.1 %gather_fusion.2 = bf16[3456,128]{1,0:T(8,128)(2,1)} fusion(bf16[1536,128]{1,0:T(8,128)(2,1)S(1)} %bitcast.33, s32[4096]{0:T(1024)S(1)} %pad_clamp_fusion), kind=kCustom, calls=%fused_computation.2 | custom fusion | bytes 1783296 | tf_op jit(solution)/shard_map/jit(_take)/gather | solution.py:273
  84.8 0.0 copy-start.1
  84.8 1.2 copy-done.1
  86.0 7.3 %shard_map.104 = (bf16[1024,128]{1,0:T(8,128)(2,1)S(1)}, f32[3456,128]{1,0:T(8,128)S(1)}) custom-call(bf16[6,6,6,16,128]{4,3,2,1,0:T(8,128)(2,1)S(1)} %bitcast.25, bf16[1024,128]{1,0:T(8,128)(2,1)S(1)} %bitcast.30, bf16[3456,128]{1,0:T(8,128)(2,1)S(1)} %get-tuple-element.21.w_second), custom_call_target="tpu_custom_call" | custom-call | tf_op jit(solution)/shard_map/pallas_call | solution.py:226
  93.2 0.7 copy.34
  94.0 0.2 pad.18.second
  94.2 22.7 %shard_map.105 = (f32[224,128]{1,0:T(8,128)S(1)}, f32[224,128]{1,0:T(8,128)S(1)}) custom-call(f32[16,224,128]{2,1,0:T(8,128)S(1)} %pad.17.first, f32[16,224,128]{2,1,0:T(8,128)S(1)} %pad.18.second), custom_call_target="tpu_custom_call" | custom-call | tf_op jit(solution)/shard_map/pallas_call | solution.py:135
  116.9 0.7 slice.50
  117.5 0.7 slice.51
  (9 shorter events, 0.1 us)
Async XLA Ops:
  7.2 7.5 %copy-start.9 = (s32[216]{0:T(256)S(1)}, s32[216]{0:T(256)}, u32[]{:S(2)}) copy-start(s32[216]{0:T(256)} %constant.59) | copy-start | bytes 2596
  7.2 2.9 %copy-start.10 = (s32[1,8]{1,0:T(1,128)S(1)}, s32[1,8]{1,0:T(1,128)}, u32[]{:S(2)}) copy-start(s32[1,8]{1,0:T(1,128)} %param.10) | copy-start | bytes 100
  7.2 7.3 %copy-start.5 = (s32[12,27]{1,0:T(8,128)S(1)}, s32[12,27]{1,0:T(8,128)}, u32[]{:S(2)}) copy-start(s32[12,27]{1,0:T(8,128)} %param.9) | copy-start | bytes 3892
  7.2 46.8 %all-gather.2.cloned.1.call-start = ((), (), s32[]{:S(2)}) async-start(), calls=%async_computation | async-start | bytes 1880064 | tf_op jit(solution)/shard_map/all_gather | solution.py:251
  9.8 8.8 %copy-start.2 = (bf16[64,12,256]{2,0,1:T(8,128)(2,1)}, bf16[64,12,256]{2,0,1:T(8,128)(2,1)S(1)}, u32[]{:S(2)}) copy-start(bf16[64,12,256]{2,0,1:T(8,128)(2,1)S(1)} %maximum_bitcast_fusion) | copy-start | bytes 1179652
  9.9 5.5 %copy-start.8 = (s32[216]{0:T(256)S(1)}, s32[216]{0:T(256)}, u32[]{:S(2)}) copy-start(s32[216]{0:T(256)} %constant.57) | copy-start | bytes 2596
  10.1 3.1 %copy-start.3 = (pred[8,12]{0,1:T(8,128)(4,1)}, pred[8,12]{0,1:T(8,128)(4,1)S(1)}, u32[]{:S(2)}) copy-start(pred[8,12]{0,1:T(8,128)(4,1)S(1)} %iota_compare_fusion) | copy-start | bytes 292
  10.8 4.8 %collective-permute-start = (bf16[64,4,256]{2,1,0:T(4,128)(2,1)S(1)}, bf16[64,4,256]{2,1,0:T(4,128)(2,1)S(1)}, u32[]{:S(2)}, u32[]{:S(2)}) collective-permute-start(bf16[64,4,256]{2,1,0:T(4,128)(2,1)S(1)} %get-tuple-element.25), channel_id=1, source_target_pairs={{0,1},{1,2},{2,3},{3,4},{4,5},{5,6},{6,7},{7,8},{8,9},{9,10},{10,1... | collective-permute-start | bytes 393224 | tf_op jit(solution)/shard_map/ppermute | solution.py:32
  13.2 5.4 %collective-permute-start.1 = (bf16[64,4,256]{2,1,0:T(4,128)(2,1)S(1)}, bf16[64,4,256]{2,1,0:T(4,128)(2,1)S(1)}, u32[]{:S(2)}, u32[]{:S(2)}) collective-permute-start(bf16[64,4,256]{2,1,0:T(4,128)(2,1)S(1)} %get-tuple-element.26), channel_id=1, source_target_pairs={{1,0},{2,1},{3,2},{4,3},{5,4},{6,5},{7,6},{8,7},{9,8},{10,9},{11,1... | collective-permute-start | bytes 393224 | tf_op jit(solution)/shard_map/ppermute | solution.py:33
  15.7 3.0 %copy-start.6 = (bf16[24]{0:T(256)(128)(2,1)}, bf16[24]{0:T(256)(128)(2,1)S(1)}, u32[]{:S(2)}) copy-start(bf16[24]{0:T(256)(128)(2,1)S(1)} %pad.26.clone) | copy-start | bytes 148
  58.7 1.2 copy-start
  59.9 10.7 %copy-start.4 = (pred[8,12]{0,1:T(8,128)(4,1)S(1)}, pred[8,12]{0,1:T(8,128)(4,1)}, u32[]{:S(2)}) copy-start(pred[8,12]{0,1:T(8,128)(4,1)} %copy-done.3) | copy-start | bytes 292
  59.9 14.8 %slice-start = ((bf16[64,12,256]{2,0,1:T(8,128)(2,1)}), bf16[64,12,128]{2,0,1:T(8,128)(2,1)S(1)}, s32[]{:S(2)}) async-start(bf16[64,12,256]{2,0,1:T(8,128)(2,1)} %copy-done.2), calls=%async_computation.1 | async-start | bytes 393216 | tf_op jit(solution)/shard_map/slice | solution.py:294
  71.2 3.9 %collective-permute-start.2 = (bf16[64,4,128]{2,1,0:T(4,128)(2,1)S(1)}, bf16[64,4,128]{2,1,0:T(4,128)(2,1)S(1)}, u32[]{:S(2)}, u32[]{:S(2)}) collective-permute-start(bf16[64,4,128]{2,1,0:T(4,128)(2,1)S(1)} %get-tuple-element.27), channel_id=1, source_target_pairs={{0,1},{1,2},{2,3},{3,4},{4,5},{5,6},{6,7},{7,8},{8,9},{9,10},{10,1... | collective-permute-start | bytes 196616 | tf_op jit(solution)/shard_map/ppermute | solution.py:32
  73.4 3.1 %collective-permute-start.3 = (bf16[64,4,128]{2,1,0:T(4,128)(2,1)S(1)}, bf16[64,4,128]{2,1,0:T(4,128)(2,1)S(1)}, u32[]{:S(2)}, u32[]{:S(2)}) collective-permute-start(bf16[64,4,128]{2,1,0:T(4,128)(2,1)S(1)} %get-tuple-element.28), channel_id=1, source_target_pairs={{1,0},{2,1},{3,2},{4,3},{5,4},{6,5},{7,6},{8,7},{9,8},{10,9},{11,1... | collective-permute-start | bytes 196616 | tf_op jit(solution)/shard_map/ppermute | solution.py:33
  74.9 1.6 %copy-start.7 = (bf16[24]{0:T(256)(128)(2,1)S(1)}, bf16[24]{0:T(256)(128)(2,1)}, u32[]{:S(2)}) copy-start(bf16[24]{0:T(256)(128)(2,1)} %copy-done.6) | copy-start | bytes 148
  84.8 1.2 copy-start.1
Sparse Core Ops, SparseCore 0:
  10.8 43.1 all-gather.1

commit v4 on v3

--- a/solution.py
+++ b/solution.py
@@ -186,7 +186,12 @@
     lax.fori_loop(0, win.shape[1] // wide, step, 0)
 
 
-def first_kernel(feats, cots, w_first, flipped, hidden, term, win, back, grad_mid):
+def first_kernel(feats, cots, both_w, hidden, term, win, back, grad_mid, flipped):
+    channels = term.shape[1]
+    for offset in range(27):
+        flipped[offset * channels : (offset + 1) * channels, :] = both_w[
+            (26 - offset) * channels : (27 - offset) * channels, channels:
+        ].T
     fill_windows(win, cots)
 
     def backward(rows):
@@ -196,7 +201,7 @@
     fill_windows(win, feats)
 
     def forward(rows):
-        first_sum = jnp.dot(win[rows, :], w_first[...], preferred_element_type=jnp.float32)
+        first_sum = jnp.dot(win[rows, :], both_w[:, :channels], preferred_element_type=jnp.float32)
         gate = jax.nn.sigmoid(first_sum)
         hidden[rows, :] = (first_sum * gate).astype(hidden.dtype)
         grad_mid[rows, :] = (
@@ -207,12 +212,27 @@
     kernel_gradient(win, grad_mid, term)
 
 
-def second_kernel(mids, cots, w_second, out_map, term, win):
-    fill_windows(win, mids)
+def fill_halo(padded, extended, choose):
+    wide = BS + 2
+    brick, local = halo_tables(BS)
+    for voxel in range(BS**3):
+        places = [p for p in range(wide**3) if local[p] == voxel]
+        rows = jnp.concatenate([choose[int(brick[p])] for p in places], axis=0)
+        got = jnp.dot(rows, extended[voxel], preferred_element_type=jnp.float32)
+        for k, p in enumerate(places):
+            padded[p // (wide * wide), p // wide % wide, p % wide] = got[
+                k * SLOTS : (k + 1) * SLOTS
+            ].astype(padded.dtype)
+
+
+def second_kernel(extended, cots, both_w, choose, out_map, term, win, padded):
+    channels = term.shape[1]
+    fill_halo(padded, extended, choose)
+    fill_windows(win, padded)
 
     def forward(rows):
         out_map[rows, :] = jnp.dot(
-            win[rows, :], w_second[...], preferred_element_type=jnp.float32
+            win[rows, :], both_w[:, channels:], preferred_element_type=jnp.float32
         ).astype(out_map.dtype)
 
     row_tiles(win, forward)
@@ -220,7 +240,8 @@
 
 
 def local_call(body, operands, extra):
-    depth, channels = operands[2].shape
+    depth = operands[2].shape[0]
+    channels = operands[2].shape[1] // 2
     rows = BS**3 * SLOTS
     whole = pl.BlockSpec(memory_space=pltpu.VMEM)
     return pl.pallas_call(
@@ -232,7 +253,7 @@
         in_specs=[whole] * len(operands),
         out_specs=[whole] * 2,
         scratch_shapes=[pltpu.VMEM((rows, depth), jnp.bfloat16)]
-        + [pltpu.VMEM((rows, channels), kind) for kind in extra],
+        + [pltpu.VMEM(shape, kind) for shape, kind in extra],
         compiler_params=pltpu.CompilerParams(vmem_limit_bytes=40 * 1024 * 1024),
     )(*operands)
 
@@ -242,7 +263,7 @@
     rim_count = rim_slots.shape[1] // 2
     chosen = rim_slots[0][:, None] == jnp.arange(capacity)[None, :]
     zero_slot = capacity + 2 * rim_count
-    width = zero_slot + 4
+    width = -(-(zero_slot + 1) // 16) * 16
     brick, local = halo_tables(BS)
 
     own_w, features, cotangent = lax.optimization_barrier(
@@ -255,7 +276,7 @@
     ).T
     index = (jnp.take(table, brick, axis=0) + jnp.asarray(local)[:, None] * width).reshape(-1)
 
-    def halo(blocks):
+    def extend(blocks):
         live = blocks[:, :capacity]
         packed = jnp.sum(
             jnp.where(chosen[None, :, :, None], live[:, None], 0), axis=2, dtype=jnp.float32
@@ -270,31 +291,32 @@
             ],
             axis=1,
         )
-        picked = jnp.take(
-            extended.reshape(-1, blocks.shape[2]), index, axis=0, mode="clip"
-        )
-        wide = BS + 2
-        return picked.reshape(wide, wide, wide, SLOTS, blocks.shape[2])
+        return extended
 
     stacked = jnp.concatenate([features, cotangent], axis=2).transpose(1, 0, 2)
-    outer = halo(stacked)
-    full_first, full_second = (both_w[:, :channels], both_w[:, channels:])
-    kernel_count = full_second.shape[0] // channels
-    flipped = (
-        full_second.reshape(kernel_count, channels, channels)[::-1]
-        .transpose(0, 2, 1)
-        .reshape(-1, channels)
-    )
+    wide = BS + 2
+    outer = jnp.take(
+        extend(stacked).reshape(-1, 2 * channels), index, axis=0, mode="clip"
+    ).reshape(wide, wide, wide, SLOTS, 2 * channels)
+    rows = vox_count * SLOTS
     hidden, term_first = local_call(
         first_kernel,
-        (outer[..., :channels], outer[..., channels:], full_first, flipped),
-        (jnp.float32, jnp.bfloat16),
+        (outer[..., :channels], outer[..., channels:], both_w),
+        (
+            ((rows, channels), jnp.float32),
+            ((rows, channels), jnp.bfloat16),
+            ((both_w.shape[0], channels), jnp.bfloat16),
+        ),
     )
     cot_rows = jnp.pad(
         stacked[..., channels:], ((0, 0), (0, SLOTS - capacity), (0, 0))
     ).reshape(-1, channels)
-    middle = halo(hidden.reshape(vox_count, SLOTS, channels))
-    out_map, term_second = local_call(second_kernel, (middle, cot_rows, full_second), ())
+    choose = (table[:, :, None] == jnp.arange(width)).astype(jnp.bfloat16)
+    out_map, term_second = local_call(
+        second_kernel,
+        (extend(hidden.reshape(vox_count, SLOTS, channels)), cot_rows, both_w, choose),
+        (((wide, wide, wide, SLOTS, channels), jnp.bfloat16),),
+    )
     out_map = out_map.reshape(vox_count, SLOTS, channels)[:, :capacity].transpose(1, 0, 2)
     grad_first, grad_second = reduce_both(term_first, term_second)
     return (out_map, grad_first, grad_second)

time: 125 us -> 112 us (0.90)
  local copies, waits for them, and re-layouts: 32.3 us -> 17.2 us
  waiting for transfers between devices: 26.4 us -> 27.7 us
    gather x2 -> x1, local copies, waits for them, and re-layouts: 19 us -> 10.6 us  [on_device(): jnp.take(extend(stacked).reshape(-1, 2 * channels), index, axis=0, mode='...]
    transpose x2 -> x0, local copies, waits for them, and re-layouts: 3.18 us -> none  [on_device(): flipped = full_second.reshape(kernel_count, channels, channels)[::-1].tra...]
    slice x1 -> x0, local copies, waits for them, and re-layouts: 1.55 us -> none  [on_device(): full_first, full_second = (both_w[:, :channels], both_w[:, channels:])]
    all_gather x1, waiting for transfers between devices: 22.1 us -> 23.5 us  [on_device(): both_w = lax.all_gather(own_w, 'tx', axis=0, tiled=True)]
    slice x1, local copies, waits for them, and re-layouts: 1.75 us -> 0.41 us  [on_device(): outer[..., channels:]]
  transfers between devices with their start and end apart: 5 -> 5, of which waited for: 3 -> 3; matrix products, arithmetic and copies ran while one was open for 13% -> 14% of each run, Pallas kernels for 0% -> 0%
where the time goes in v4:
time: 112 us
  Pallas kernels  41.3 us (37%)
  waiting for transfers between devices  27.7 us (25%)
  local copies, waits for them, and re-layouts  17.2 us (15%)
  between operations  14.4 us (13%)
  starting transfers between devices  7.14 us (6%)
  other arithmetic  4.28 us (4%)
    all_gather x1, waiting for transfers between devices, on_device(): both_w = lax.all_gather(own_w, 'tx', axis=0, tiled=True)  23.5 us
    pallas_call x1, Pallas kernels, reduce_both(): pl.pallas_call(functools.partial(halving_kernel, size, bit_orders(size)),...  22.7 us
    pallas_call x2, Pallas kernels, local_call(): pl.pallas_call(body, out_shape=[jax.ShapeDtypeStruct((rows, channels), jn...  18.6 us
    gather x1, local copies, waits for them, and re-layouts, on_device(): jnp.take(extend(stacked).reshape(-1, 2 * channels), index, axis=0, mode='...  10.6 us
    ppermute x2, starting transfers between devices, neighbours(): before = lax.ppermute(packed[:, rim_count:], 'tx', up)  4.52 us
    ppermute x2, waiting for transfers between devices, neighbours(): after = lax.ppermute(packed[:, :rim_count], 'tx', down)  4.16 us
    ppermute x2, starting transfers between devices, neighbours(): after = lax.ppermute(packed[:, :rim_count], 'tx', down)  2.58 us
    unnamed x25, local copies, waits for them, and re-layouts  2.49 us
  transfers between devices with their start and end apart: 5, of which 3 were waited for; matrix products, arithmetic and copies ran while one was open for 14% of the time, Pallas kernels for 0%

profile of v4, /device:TPU:0, one launch (start us, length us, event | category | flops | bytes accessed | tf_op | source)
XLA Modules:
  0.0 112.0 jit_solution(13356881004230793692)
XLA Ops:
  7.2 0.0 copy-start.9
  7.2 0.0 copy-start.10
  7.2 0.0 copy-start.5
  7.2 0.0 all-gather.2.cloned.1.call-start
  7.2 1.5 %pad_maximum_fusion = bf16[216,256]{1,0:T(8,128)(2,1)} fusion(bf16[216,128]{1,0:T(8,128)(2,1)} %param.12, bf16[216,128]{1,0:T(8,128)(2,1)} %param.11), kind=kLoop, calls=%fused_computation.10 | loop fusion | flops 221184 | bytes 221184 | tf_op jit(solution)/shard_map/concatenate | solution.py:270
  8.7 0.0 all-gather.2.cloned.1.call-update
  8.8 1.1 maximum_bitcast_fusion
  9.8 0.0 copy-start.2
  9.9 0.0 copy-start.8
  9.9 0.2 copy.21
  10.1 0.0 copy-done.10
  10.1 0.0 copy-start.3
  10.1 0.6 select_reduce_fusion
  10.8 0.1 fusion.2
  10.8 2.4 %collective-permute-start = (bf16[64,4,256]{2,1,0:T(4,128)(2,1)S(1)}, bf16[64,4,256]{2,1,0:T(4,128)(2,1)S(1)}, u32[]{:S(2)}, u32[]{:S(2)}) collective-permute-start(bf16[64,4,256]{2,1,0:T(4,128)(2,1)S(1)} %get-tuple-element.23), channel_id=1, source_target_pairs={{0,1},{1,2},{2,3},{3,4},{4,5},{5,6},{6,7},{7,8},{8,9},{9,10},{10,1... | collective-permute-start | bytes 393224 | tf_op jit(solution)/shard_map/ppermute | solution.py:32
  13.2 0.0 copy-done.3
  13.2 1.3 %collective-permute-start.1 = (bf16[64,4,256]{2,1,0:T(4,128)(2,1)S(1)}, bf16[64,4,256]{2,1,0:T(4,128)(2,1)S(1)}, u32[]{:S(2)}, u32[]{:S(2)}) collective-permute-start(bf16[64,4,256]{2,1,0:T(4,128)(2,1)S(1)} %get-tuple-element.24), channel_id=1, source_target_pairs={{1,0},{2,1},{3,2},{4,3},{5,4},{6,5},{7,6},{8,7},{9,8},{10,9},{11,1... | collective-permute-start | bytes 393224 | tf_op jit(solution)/shard_map/ppermute | solution.py:33
  14.5 0.0 copy-done.5
  14.5 0.1 copy.25
  14.6 0.0 copy-done.9
  14.7 0.7 gather_fusion
  15.4 0.0 copy-done.8
  15.4 0.1 broadcast_add_fusion
  15.5 0.1 reshape.113
  15.6 0.1 pad.26.clone
  15.7 0.0 copy-start.6
  15.7 0.0 collective-permute-done
  15.7 2.9 %collective-permute-done.1 = bf16[64,4,256]{2,1,0:T(4,128)(2,1)S(1)} collective-permute-done((bf16[64,4,256]{2,1,0:T(4,128)(2,1)S(1)}, bf16[64,4,256]{2,1,0:T(4,128)(2,1)S(1)}, u32[]{:S(2)}, u32[]{:S(2)}) %collective-permute-start.1) | collective-permute-done | bytes 131104 | tf_op jit(solution)/shard_map/ppermute | solution.py:33
  18.6 0.0 copy-done.2
  18.6 0.0 copy-done.6
  18.6 0.1 maximum_maximum_fusion
  18.8 0.6 copy.24
  19.4 10.6 %gather_fusion.1 = bf16[3456,256]{1,0:T(8,128)(2,1)S(1)} fusion(bf16[2048,256]{1,0:T(8,128)(2,1)S(1)} %bitcast.23, s32[4096]{0:T(1024)S(1)} %pad_clamp_fusion), kind=kCustom, calls=%fused_computation.1 | custom fusion | bytes 3552768 | tf_op jit(solution)/shard_map/jit(_take)/gather | solution.py:298
  30.0 0.4 fusion.1
  30.5 23.5 %all-gather.2.cloned.1.call-done.both_w = bf16[3456,256]{1,0:T(8,128)(2,1)} async-done(((bf16[216,256]{1,0:T(8,128)(2,1)}), bf16[3456,256]{1,0:T(8,128)(2,1)}) %all-gather.2.cloned.1.call-update) | async-done | bytes 1769488 | tf_op jit(solution)/shard_map/all_gather | solution.py:272
  54.0 0.0 copy-start
  54.0 1.5 %copy-done = bf16[3456,256]{1,0:T(8,128)(2,1)S(1)} copy-done((bf16[3456,256]{1,0:T(8,128)(2,1)S(1)}, bf16[3456,256]{1,0:T(8,128)(2,1)}, u32[]{:S(2)}) %copy-start) | copy-done | bytes 1769496
  55.5 0.0 copy-start.4
  55.5 0.0 slice-start
  55.5 10.9 %shard_map.103 = (bf16[1024,128]{1,0:T(8,128)(2,1)S(1)}, f32[3456,128]{1,0:T(8,128)S(1)}) custom-call(bf16[6,6,6,16,128]{4,3,2,1,0:T(8,128)(2,1)S(1)} %get-tuple-element.22.feats, bf16[6,6,6,16,128]{4,3,2,1,0:T(8,128)(2,1)S(1)} %get-tuple-element.21.cots, bf16[3456,256]{1,0:T(8,128)(2,1)S(1)} %copy-done), custom_call_target="tpu_custom_call" | custom-call | tf_op jit(solution)/shard_map/pallas_call | solution.py:247
  66.4 0.0 copy-done.4
  66.4 0.5 select_reduce_fusion.1
  67.0 2.2 %collective-permute-start.2 = (bf16[64,4,128]{2,1,0:T(4,128)(2,1)S(1)}, bf16[64,4,128]{2,1,0:T(4,128)(2,1)S(1)}, u32[]{:S(2)}, u32[]{:S(2)}) collective-permute-start(bf16[64,4,128]{2,1,0:T(4,128)(2,1)S(1)} %get-tuple-element.25), channel_id=1, source_target_pairs={{0,1},{1,2},{2,3},{3,4},{4,5},{5,6},{6,7},{7,8},{8,9},{9,10},{10,1... | collective-permute-start | bytes 196616 | tf_op jit(solution)/shard_map/ppermute | solution.py:32
  69.1 1.3 %collective-permute-start.3 = (bf16[64,4,128]{2,1,0:T(4,128)(2,1)S(1)}, bf16[64,4,128]{2,1,0:T(4,128)(2,1)S(1)}, u32[]{:S(2)}, u32[]{:S(2)}) collective-permute-start(bf16[64,4,128]{2,1,0:T(4,128)(2,1)S(1)} %get-tuple-element.26), channel_id=1, source_target_pairs={{1,0},{2,1},{3,2},{4,3},{5,4},{6,5},{7,6},{8,7},{9,8},{10,9},{11,1... | collective-permute-start | bytes 196616 | tf_op jit(solution)/shard_map/ppermute | solution.py:33
  70.4 0.1 fusion.choose
  70.6 0.0 slice-done
  70.6 0.1 copy.29
  70.7 0.1 pad.16.clone
  70.8 0.0 copy-start.7
  70.8 0.0 copy-start.1
  70.8 0.2 pad.17.first
  71.0 0.0 collective-permute-done.2
  71.0 1.3 %collective-permute-done.3 = bf16[64,4,128]{2,1,0:T(4,128)(2,1)S(1)} collective-permute-done((bf16[64,4,128]{2,1,0:T(4,128)(2,1)S(1)}, bf16[64,4,128]{2,1,0:T(4,128)(2,1)S(1)}, u32[]{:S(2)}, u32[]{:S(2)}) %collective-permute-start.3) | collective-permute-done | bytes 65568 | tf_op jit(solution)/shard_map/ppermute | solution.py:33
  72.3 0.0 copy-done.7
  72.3 0.2 maximum_maximum_fusion.1.extended
  72.5 0.0 copy-done.1
  72.5 7.7 %shard_map.104 = (bf16[1024,128]{1,0:T(8,128)(2,1)S(1)}, f32[3456,128]{1,0:T(8,128)S(1)}) custom-call(bf16[64,32,128]{2,1,0:T(8,128)(2,1)S(1)} %maximum_maximum_fusion.1.extended, bf16[1024,128]{1,0:T(8,128)(2,1)S(1)} %bitcast.21, bf16[3456,256]{1,0:T(8,128)(2,1)S(1)} %copy-done.1, bf16[27,16,32]{2,1,0:T(8,128)(2,1)S(1)} %fusion.choose), custom_call_target="tpu_custom_call" | custom-call | tf_op jit(solution)/shard_map/pallas_call | solution.py:247
  80.2 0.2 pad.18.second
  80.4 22.7 %shard_map.105 = (f32[224,128]{1,0:T(8,128)S(1)}, f32[224,128]{1,0:T(8,128)S(1)}) custom-call(f32[16,224,128]{2,1,0:T(8,128)S(1)} %pad.17.first, f32[16,224,128]{2,1,0:T(8,128)S(1)} %pad.18.second), custom_call_target="tpu_custom_call" | custom-call | tf_op jit(solution)/shard_map/pallas_call | solution.py:135
  103.1 0.7 slice.42
  103.8 0.7 slice.43
  104.4 0.7 copy.31
  (8 shorter events, 0.1 us)
Async XLA Ops:
  7.2 7.5 %copy-start.9 = (s32[216]{0:T(256)S(1)}, s32[216]{0:T(256)}, u32[]{:S(2)}) copy-start(s32[216]{0:T(256)} %constant.59) | copy-start | bytes 2596
  7.2 2.9 %copy-start.10 = (s32[1,8]{1,0:T(1,128)S(1)}, s32[1,8]{1,0:T(1,128)}, u32[]{:S(2)}) copy-start(s32[1,8]{1,0:T(1,128)} %param.10) | copy-start | bytes 100
  7.2 7.3 %copy-start.5 = (s32[12,27]{1,0:T(8,128)S(1)}, s32[12,27]{1,0:T(8,128)}, u32[]{:S(2)}) copy-start(s32[12,27]{1,0:T(8,128)} %param.9) | copy-start | bytes 3892
  7.2 46.8 %all-gather.2.cloned.1.call-start = ((), (), s32[]{:S(2)}) async-start(), calls=%async_computation | async-start | bytes 1880064 | tf_op jit(solution)/shard_map/all_gather | solution.py:272
  9.8 8.8 %copy-start.2 = (bf16[64,12,256]{2,0,1:T(8,128)(2,1)}, bf16[64,12,256]{2,0,1:T(8,128)(2,1)S(1)}, u32[]{:S(2)}) copy-start(bf16[64,12,256]{2,0,1:T(8,128)(2,1)S(1)} %maximum_bitcast_fusion) | copy-start | bytes 1179652
  9.9 5.5 %copy-start.8 = (s32[216]{0:T(256)S(1)}, s32[216]{0:T(256)}, u32[]{:S(2)}) copy-start(s32[216]{0:T(256)} %constant.57) | copy-start | bytes 2596
  10.1 3.1 %copy-start.3 = (pred[8,12]{0,1:T(8,128)(4,1)}, pred[8,12]{0,1:T(8,128)(4,1)S(1)}, u32[]{:S(2)}) copy-start(pred[8,12]{0,1:T(8,128)(4,1)S(1)} %iota_compare_fusion.1) | copy-start | bytes 292
  10.8 4.8 %collective-permute-start = (bf16[64,4,256]{2,1,0:T(4,128)(2,1)S(1)}, bf16[64,4,256]{2,1,0:T(4,128)(2,1)S(1)}, u32[]{:S(2)}, u32[]{:S(2)}) collective-permute-start(bf16[64,4,256]{2,1,0:T(4,128)(2,1)S(1)} %get-tuple-element.23), channel_id=1, source_target_pairs={{0,1},{1,2},{2,3},{3,4},{4,5},{5,6},{6,7},{7,8},{8,9},{9,10},{10,1... | collective-permute-start | bytes 393224 | tf_op jit(solution)/shard_map/ppermute | solution.py:32
  13.2 5.4 %collective-permute-start.1 = (bf16[64,4,256]{2,1,0:T(4,128)(2,1)S(1)}, bf16[64,4,256]{2,1,0:T(4,128)(2,1)S(1)}, u32[]{:S(2)}, u32[]{:S(2)}) collective-permute-start(bf16[64,4,256]{2,1,0:T(4,128)(2,1)S(1)} %get-tuple-element.24), channel_id=1, source_target_pairs={{1,0},{2,1},{3,2},{4,3},{5,4},{6,5},{7,6},{8,7},{9,8},{10,9},{11,1... | collective-permute-start | bytes 393224 | tf_op jit(solution)/shard_map/ppermute | solution.py:33
  15.7 3.0 %copy-start.6 = (bf16[32]{0:T(256)(128)(2,1)}, bf16[32]{0:T(256)(128)(2,1)S(1)}, u32[]{:S(2)}) copy-start(bf16[32]{0:T(256)(128)(2,1)S(1)} %pad.26.clone) | copy-start | bytes 196
  54.0 1.5 %copy-start = (bf16[3456,256]{1,0:T(8,128)(2,1)S(1)}, bf16[3456,256]{1,0:T(8,128)(2,1)}, u32[]{:S(2)}) copy-start(bf16[3456,256]{1,0:T(8,128)(2,1)} %all-gather.2.cloned.1.call-done.both_w) | copy-start | bytes 5308420
  55.5 10.9 %copy-start.4 = (pred[8,12]{0,1:T(8,128)(4,1)S(1)}, pred[8,12]{0,1:T(8,128)(4,1)}, u32[]{:S(2)}) copy-start(pred[8,12]{0,1:T(8,128)(4,1)} %copy-done.3) | copy-start | bytes 292
  55.5 15.1 %slice-start = ((bf16[64,12,256]{2,0,1:T(8,128)(2,1)}), bf16[64,12,128]{2,0,1:T(8,128)(2,1)S(1)}, s32[]{:S(2)}) async-start(bf16[64,12,256]{2,0,1:T(8,128)(2,1)} %copy-done.2), calls=%async_computation.1 | async-start | bytes 393216 | tf_op jit(solution)/shard_map/slice | solution.py:312
  67.0 4.0 %collective-permute-start.2 = (bf16[64,4,128]{2,1,0:T(4,128)(2,1)S(1)}, bf16[64,4,128]{2,1,0:T(4,128)(2,1)S(1)}, u32[]{:S(2)}, u32[]{:S(2)}) collective-permute-start(bf16[64,4,128]{2,1,0:T(4,128)(2,1)S(1)} %get-tuple-element.25), channel_id=1, source_target_pairs={{0,1},{1,2},{2,3},{3,4},{4,5},{5,6},{6,7},{7,8},{8,9},{9,10},{10,1... | collective-permute-start | bytes 196616 | tf_op jit(solution)/shard_map/ppermute | solution.py:32
  69.1 3.1 %collective-permute-start.3 = (bf16[64,4,128]{2,1,0:T(4,128)(2,1)S(1)}, bf16[64,4,128]{2,1,0:T(4,128)(2,1)S(1)}, u32[]{:S(2)}, u32[]{:S(2)}) collective-permute-start(bf16[64,4,128]{2,1,0:T(4,128)(2,1)S(1)} %get-tuple-element.26), channel_id=1, source_target_pairs={{1,0},{2,1},{3,2},{4,3},{5,4},{6,5},{7,6},{8,7},{9,8},{10,9},{11,1... | collective-permute-start | bytes 196616 | tf_op jit(solution)/shard_map/ppermute | solution.py:33
  70.8 1.5 %copy-start.7 = (bf16[32]{0:T(256)(128)(2,1)S(1)}, bf16[32]{0:T(256)(128)(2,1)}, u32[]{:S(2)}) copy-start(bf16[32]{0:T(256)(128)(2,1)} %copy-done.6) | copy-start | bytes 196
  70.8 1.7 %copy-start.1 = (bf16[3456,256]{1,0:T(8,128)(2,1)S(1)}, bf16[3456,256]{1,0:T(8,128)(2,1)}, u32[]{:S(2)}) copy-start(bf16[3456,256]{1,0:T(8,128)(2,1)} %all-gather.2.cloned.1.call-done.both_w) | copy-start | bytes 5308420
Sparse Core Ops, SparseCore 0:
  10.8 43.1 all-gather.1

commit v5 on v4

--- a/solution.py
+++ b/solution.py
@@ -118,6 +118,74 @@
     for stream in range(2):
         for copy in copies[stream]:
             copy.wait_send()
+
+
+def doubling_kernel(size, orders, first, second, out_first, out_second, send_sem, recv_sem):
+    steps = size.bit_length() - 1
+    me = lax.axis_index("tx")
+    barrier = pltpu.get_barrier_semaphore()
+
+    def moved(mask):
+        place = me
+        for bit in range(steps):
+            if mask >> bit & 1:
+                place = place + (1 - 2 * (me // (1 << bit) % 2)) * (1 << bit)
+        return place
+
+    out_first[me] = first[...]
+    out_second[me] = second[...]
+    for bit in range(steps):
+        pl.semaphore_signal(
+            barrier, inc=1, device_id={"tx": moved(1 << bit)}, device_id_type=pl.DeviceIdType.MESH
+        )
+    pl.semaphore_wait(barrier, steps)
+    outs = (out_first, out_second)
+    known = [[0], [0]]
+    latest = [[], []]
+    copies = []
+    for step in range(steps):
+        for stream in range(2):
+            bit = orders[stream][steps - 1 - step]
+            for copy in latest[stream]:
+                copy.wait_recv()
+            latest[stream] = []
+            for mask in known[stream]:
+                slot = mask | 1 << bit
+                copy = pltpu.make_async_remote_copy(
+                    src_ref=outs[stream].at[moved(mask)],
+                    dst_ref=outs[stream].at[moved(mask)],
+                    send_sem=send_sem.at[stream, slot],
+                    recv_sem=recv_sem.at[stream, slot],
+                    device_id={"tx": moved(1 << bit)},
+                    device_id_type=pl.DeviceIdType.MESH,
+                )
+                copy.start()
+                latest[stream].append(copy)
+            copies += latest[stream]
+            known[stream] = known[stream] + [mask | 1 << bit for mask in known[stream]]
+    for stream in range(2):
+        for copy in latest[stream]:
+            copy.wait_recv()
+    for copy in copies:
+        copy.wait_send()
+
+
+def gather_both(first, second):
+    size = lax.axis_size("tx")
+    rows, lanes = first.shape
+    tall = -(-rows // 16) * 16
+    whole = pl.BlockSpec(memory_space=pltpu.VMEM)
+    outs = pl.pallas_call(
+        functools.partial(doubling_kernel, size, bit_orders(size)),
+        out_shape=[jax.ShapeDtypeStruct((size, tall, lanes), first.dtype)] * 2,
+        in_specs=[whole] * 2,
+        out_specs=[whole] * 2,
+        scratch_shapes=[pltpu.SemaphoreType.DMA((2, size)), pltpu.SemaphoreType.DMA((2, size))],
+        compiler_params=pltpu.CompilerParams(
+            collective_id=1, has_side_effects=True, vmem_limit_bytes=16 * 1024 * 1024
+        ),
+    )(*(jnp.pad(x, ((0, tall - rows), (0, 0))) for x in (first, second)))
+    return jnp.concatenate([x[:, :rows].reshape(-1, lanes) for x in outs], axis=1)
 
 
 def reduce_both(first, second):
@@ -150,12 +218,11 @@
 CONTRACT = (((0,), (0,)), ((), ()))
 
 
-def fill_windows(win, padded):
-    channels = padded.shape[-1]
+def fill_windows(win, padded, lane, channels):
     for offset in range(27):
         a, b, c = (offset // 9, offset // 3 % 3, offset % 3)
         for i in range(BS):
-            part = padded[a + i, b : b + BS, c : c + BS]
+            part = padded[a + i, b : b + BS, c : c + BS, :, lane : lane + channels]
             rows = BS * BS * SLOTS
             win[i * rows : (i + 1) * rows, offset * channels : (offset + 1) * channels] = (
                 part.reshape(rows, channels)
@@ -186,19 +253,20 @@
     lax.fori_loop(0, win.shape[1] // wide, step, 0)
 
 
-def first_kernel(feats, cots, both_w, hidden, term, win, back, grad_mid, flipped):
+def first_kernel(extended, choose, both_w, hidden, term, win, back, grad_mid, flipped, padded):
     channels = term.shape[1]
+    fill_halo(padded, extended, choose)
     for offset in range(27):
         flipped[offset * channels : (offset + 1) * channels, :] = both_w[
             (26 - offset) * channels : (27 - offset) * channels, channels:
         ].T
-    fill_windows(win, cots)
+    fill_windows(win, padded, channels, channels)
 
     def backward(rows):
         back[rows, :] = jnp.dot(win[rows, :], flipped[...], preferred_element_type=jnp.float32)
 
     row_tiles(win, backward)
-    fill_windows(win, feats)
+    fill_windows(win, padded, 0, channels)
 
     def forward(rows):
         first_sum = jnp.dot(win[rows, :], both_w[:, :channels], preferred_element_type=jnp.float32)
@@ -228,7 +296,7 @@
 def second_kernel(extended, cots, both_w, choose, out_map, term, win, padded):
     channels = term.shape[1]
     fill_halo(padded, extended, choose)
-    fill_windows(win, padded)
+    fill_windows(win, padded, 0, channels)
 
     def forward(rows):
         out_map[rows, :] = jnp.dot(
@@ -264,18 +332,11 @@
     chosen = rim_slots[0][:, None] == jnp.arange(capacity)[None, :]
     zero_slot = capacity + 2 * rim_count
     width = -(-(zero_slot + 1) // 16) * 16
-    brick, local = halo_tables(BS)
-
-    own_w, features, cotangent = lax.optimization_barrier(
-        (jnp.concatenate([w_first, w_second], axis=1), features, cotangent)
-    )
-    both_w = lax.all_gather(own_w, "tx", axis=0, tiled=True)
+    both_w = gather_both(w_first, w_second)
 
     table = jnp.pad(
         nbr_table, ((0, SLOTS - capacity), (0, 0)), constant_values=zero_slot
     ).T
-    index = (jnp.take(table, brick, axis=0) + jnp.asarray(local)[:, None] * width).reshape(-1)
-
     def extend(blocks):
         live = blocks[:, :capacity]
         packed = jnp.sum(
@@ -295,23 +356,21 @@
 
     stacked = jnp.concatenate([features, cotangent], axis=2).transpose(1, 0, 2)
     wide = BS + 2
-    outer = jnp.take(
-        extend(stacked).reshape(-1, 2 * channels), index, axis=0, mode="clip"
-    ).reshape(wide, wide, wide, SLOTS, 2 * channels)
+    choose = (table[:, :, None] == jnp.arange(width)).astype(jnp.bfloat16)
     rows = vox_count * SLOTS
     hidden, term_first = local_call(
         first_kernel,
-        (outer[..., :channels], outer[..., channels:], both_w),
+        (extend(stacked), choose, both_w),
         (
             ((rows, channels), jnp.float32),
             ((rows, channels), jnp.bfloat16),
             ((both_w.shape[0], channels), jnp.bfloat16),
+            ((wide, wide, wide, SLOTS, 2 * channels), jnp.bfloat16),
         ),
     )
     cot_rows = jnp.pad(
         stacked[..., channels:], ((0, 0), (0, SLOTS - capacity), (0, 0))
     ).reshape(-1, channels)
-    choose = (table[:, :, None] == jnp.arange(width)).astype(jnp.bfloat16)
     out_map, term_second = local_call(
         second_kernel,
         (extend(hidden.reshape(vox_count, SLOTS, channels)), cot_rows, both_w, choose),

time: 112 us -> 88.6 us (0.79)
  Pallas kernels: 41.3 us -> 70.6 us
  waiting for transfers between devices: 27.7 us -> 1.54 us
  between operations: 14.4 us -> 0.89 us
  local copies, waits for them, and re-layouts: 17.2 us -> 5.12 us
  other arithmetic: 4.28 us -> 2.87 us
    pallas_call x0 -> x1, Pallas kernels: none -> 25.9 us  [gather_both(): pl.pallas_call(functools.partial(doubling_kernel, size, bit_orders(size))...]
    all_gather x1 -> x0, waiting for transfers between devices: 23.5 us -> none  [on_device(): both_w = lax.all_gather(own_w, 'tx', axis=0, tiled=True)]
    gather x2 -> x0, local copies, waits for them, and re-layouts: 11.4 us -> none  [the longest x1 10.6 us: on_device(): jnp.take(extend(stacked).reshape(-1, 2 * channels), index, axis=0, mode='...]
    pallas_call x1, Pallas kernels: 22.7 us -> 25.7 us  [reduce_both(): pl.pallas_call(functools.partial(halving_kernel, size, bit_orders(size)),...]
    ppermute x2, waiting for transfers between devices: 4.16 us -> 1.53 us  [neighbours(): after = lax.ppermute(packed[:, :rim_count], 'tx', down)]
    concatenate x1, other arithmetic: 1.5 us -> 0.19 us  [gather_both(): jnp.concatenate([x[:, :rows].reshape(-1, lanes) for x in outs], axis=1)]
    unnamed x25 -> x9, local copies, waits for them, and re-layouts: 2.49 us -> 2.9 us
  transfers between devices with their start and end apart: 5 -> 4, of which waited for: 3 -> 1; matrix products, arithmetic and copies ran while one was open for 14% -> 1% of each run, Pallas kernels for 0% -> 29%
where the time goes in v5:
time: 88.6 us; the launch traced here: 88.3 us
  Pallas kernels  70.6 us (80%)
  starting transfers between devices  7.27 us (8%)
  local copies, waits for them, and re-layouts  5.12 us (6%)
  other arithmetic  2.87 us (3%)
  waiting for transfers between devices  1.54 us (2%)
  between operations  0.89 us (1%)
    pallas_call x1, Pallas kernels, gather_both(): pl.pallas_call(functools.partial(doubling_kernel, size, bit_orders(size))...  25.9 us
    pallas_call x1, Pallas kernels, reduce_both(): pl.pallas_call(functools.partial(halving_kernel, size, bit_orders(size)),...  25.7 us
    pallas_call x2, Pallas kernels, local_call(): pl.pallas_call(body, out_shape=[jax.ShapeDtypeStruct((rows, channels), jn...  19 us
    ppermute x2, starting transfers between devices, neighbours(): before = lax.ppermute(packed[:, rim_count:], 'tx', up)  4.69 us
    unnamed x9, local copies, waits for them, and re-layouts  2.9 us
    ppermute x2, starting transfers between devices, neighbours(): after = lax.ppermute(packed[:, :rim_count], 'tx', down)  2.58 us
  transfers between devices with their start and end apart: 4, of which 1 were waited for; matrix products, arithmetic and copies ran while one was open for 1% of the time, Pallas kernels for 29%

profile of v5, /device:TPU:0, one launch (start us, length us, event | category | flops | bytes accessed | tf_op | source)
XLA Modules:
  0.0 88.3 jit_solution(3803090593814583531)
XLA Ops:
  0.6 0.0 copy-start
  0.6 0.0 copy-start.1
  0.7 1.1 %copy.13 = bf16[12,64,128]{2,0,1:T(8,128)(2,1)S(1)} copy(bf16[12,64,128]{2,1,0:T(8,128)(2,1)} %param.6) | data formatting | bytes 393216 | tf_op args[0]
  1.7 1.1 %copy.14 = bf16[12,64,128]{2,0,1:T(8,128)(2,1)S(1)} copy(bf16[12,64,128]{2,1,0:T(8,128)(2,1)} %param.11) | data formatting | bytes 393216 | tf_op args[5]
  2.8 0.7 iota_compare_fusion.1
  3.5 0.1 maximum_bitcast_fusion
  3.6 0.6 select_reduce_fusion
  4.2 0.1 fusion.1
  4.3 2.4 %collective-permute-start = (bf16[64,4,256]{2,1,0:T(4,128)(2,1)S(1)}, bf16[64,4,256]{2,1,0:T(4,128)(2,1)S(1)}, u32[]{:S(2)}, u32[]{:S(2)}) collective-permute-start(bf16[64,4,256]{2,1,0:T(4,128)(2,1)S(1)} %get-tuple-element.19), channel_id=1, source_target_pairs={{0,1},{1,2},{2,3},{3,4},{4,5},{5,6},{6,7},{7,8},{8,9},{9,10},{10,1... | collective-permute-start | bytes 393224 | tf_op jit(solution)/shard_map/ppermute | solution.py:32
  6.6 1.3 %collective-permute-start.1 = (bf16[64,4,256]{2,1,0:T(4,128)(2,1)S(1)}, bf16[64,4,256]{2,1,0:T(4,128)(2,1)S(1)}, u32[]{:S(2)}, u32[]{:S(2)}) collective-permute-start(bf16[64,4,256]{2,1,0:T(4,128)(2,1)S(1)} %get-tuple-element.20), channel_id=1, source_target_pairs={{1,0},{2,1},{3,2},{4,3},{5,4},{6,5},{7,6},{8,7},{9,8},{10,9},{11,1... | collective-permute-start | bytes 393224 | tf_op jit(solution)/shard_map/ppermute | solution.py:33
  7.9 0.0 copy-done
  8.0 0.0 copy-done.1
  8.0 0.0 copy-start.2
  8.0 25.9 %shard_map.85 = (bf16[16,224,128]{2,1,0:T(8,128)(2,1)S(1)}, bf16[16,224,128]{2,1,0:T(8,128)(2,1)S(1)}) custom-call(bf16[224,128]{1,0:T(8,128)(2,1)S(1)} %pad.23.first, bf16[224,128]{1,0:T(8,128)(2,1)S(1)} %pad.24.second), custom_call_target="tpu_custom_call" | custom-call | tf_op jit(solution)/shard_map/pallas_call | solution.py:178
  33.9 0.1 slice.35
  34.0 0.1 slice.36
  34.0 0.0 copy-done.2
  34.0 0.1 copy.15
  34.1 0.1 pad.37.clone
  34.2 0.2 pad_maximum_fusion.both_w
  34.4 0.1 fusion.choose
  34.5 0.0 collective-permute-done
  34.6 0.0 collective-permute-done.1
  34.6 0.5 maximum_maximum_fusion.extended
  35.1 11.4 %shard_map.86 = (bf16[1024,128]{1,0:T(8,128)(2,1)S(1)}, f32[3456,128]{1,0:T(8,128)S(1)}) custom-call(bf16[64,32,256]{2,1,0:T(8,128)(2,1)S(1)} %maximum_maximum_fusion.extended, bf16[27,16,32]{2,1,0:T(8,128)(2,1)S(1)} %fusion.choose, bf16[3456,256]{1,0:T(8,128)(2,1)S(1)} %pad_maximum_fusion.both_w), custom_call_target="tpu_custom_call" | custom-call | tf_op jit(solution)/shard_map/pallas_call | solution.py:315
  46.4 0.5 select_reduce_fusion.1
  47.0 2.3 %collective-permute-start.2 = (bf16[64,4,128]{2,1,0:T(4,128)(2,1)S(1)}, bf16[64,4,128]{2,1,0:T(4,128)(2,1)S(1)}, u32[]{:S(2)}, u32[]{:S(2)}) collective-permute-start(bf16[64,4,128]{2,1,0:T(4,128)(2,1)S(1)} %get-tuple-element.21), channel_id=1, source_target_pairs={{0,1},{1,2},{2,3},{3,4},{4,5},{5,6},{6,7},{7,8},{8,9},{9,10},{10,1... | collective-permute-start | bytes 196616 | tf_op jit(solution)/shard_map/ppermute | solution.py:32
  49.3 1.3 %collective-permute-start.3 = (bf16[64,4,128]{2,1,0:T(4,128)(2,1)S(1)}, bf16[64,4,128]{2,1,0:T(4,128)(2,1)S(1)}, u32[]{:S(2)}, u32[]{:S(2)}) collective-permute-start(bf16[64,4,128]{2,1,0:T(4,128)(2,1)S(1)} %get-tuple-element.22), channel_id=1, source_target_pairs={{1,0},{2,1},{3,2},{4,3},{5,4},{6,5},{7,6},{8,7},{9,8},{10,9},{11,1... | collective-permute-start | bytes 196616 | tf_op jit(solution)/shard_map/ppermute | solution.py:33
  50.7 0.1 pad.25
  50.8 0.2 pad.26.first
  50.9 0.0 collective-permute-done.2
  51.0 1.5 %collective-permute-done.3 = bf16[64,4,128]{2,1,0:T(4,128)(2,1)S(1)} collective-permute-done((bf16[64,4,128]{2,1,0:T(4,128)(2,1)S(1)}, bf16[64,4,128]{2,1,0:T(4,128)(2,1)S(1)}, u32[]{:S(2)}, u32[]{:S(2)}) %collective-permute-start.3) | collective-permute-done | bytes 65568 | tf_op jit(solution)/shard_map/ppermute | solution.py:33
  52.5 0.2 maximum_maximum_fusion.1.extended
  52.7 7.7 %shard_map.87 = (bf16[1024,128]{1,0:T(8,128)(2,1)S(1)}, f32[3456,128]{1,0:T(8,128)S(1)}) custom-call(bf16[64,32,128]{2,1,0:T(8,128)(2,1)S(1)} %maximum_maximum_fusion.1.extended, bf16[1024,128]{1,0:T(8,128)(2,1)S(1)} %bitcast.21, bf16[3456,256]{1,0:T(8,128)(2,1)S(1)} %pad_maximum_fusion.both_w, bf16[27,16,32]{2,1,0:T(8,128)(2,1)S(1)} %fusion.choose), custom_call_target="tpu_custom_call" | custom-call | tf_op jit(solution)/shard_map/pallas_call | solution.py:315
  60.4 0.2 pad.27.second
  60.6 25.7 %shard_map.88 = (f32[224,128]{1,0:T(8,128)S(1)}, f32[224,128]{1,0:T(8,128)S(1)}) custom-call(f32[16,224,128]{2,1,0:T(8,128)S(1)} %pad.26.first, f32[16,224,128]{2,1,0:T(8,128)S(1)} %pad.27.second), custom_call_target="tpu_custom_call" | custom-call | tf_op jit(solution)/shard_map/pallas_call | solution.py:203
  86.3 0.7 slice.42
  86.9 0.7 slice.43
  87.6 0.7 copy.19
  (6 shorter events, 0.1 us)
Async XLA Ops:
  0.6 7.3 %copy-start = (bf16[216,128]{1,0:T(8,128)(2,1)S(1)}, bf16[216,128]{1,0:T(8,128)(2,1)}, u32[]{:S(2)}) copy-start(bf16[216,128]{1,0:T(8,128)(2,1)} %param.9) | copy-start | bytes 165892
  0.6 7.3 %copy-start.1 = (bf16[216,128]{1,0:T(8,128)(2,1)S(1)}, bf16[216,128]{1,0:T(8,128)(2,1)}, u32[]{:S(2)}) copy-start(bf16[216,128]{1,0:T(8,128)(2,1)} %param.10) | copy-start | bytes 165892
  4.3 30.3 %collective-permute-start = (bf16[64,4,256]{2,1,0:T(4,128)(2,1)S(1)}, bf16[64,4,256]{2,1,0:T(4,128)(2,1)S(1)}, u32[]{:S(2)}, u32[]{:S(2)}) collective-permute-start(bf16[64,4,256]{2,1,0:T(4,128)(2,1)S(1)} %get-tuple-element.19), channel_id=1, source_target_pairs={{0,1},{1,2},{2,3},{3,4},{4,5},{5,6},{6,7},{7,8},{8,9},{9,10},{10,1... | collective-permute-start | bytes 393224 | tf_op jit(solution)/shard_map/ppermute | solution.py:32
  6.6 27.9 %collective-permute-start.1 = (bf16[64,4,256]{2,1,0:T(4,128)(2,1)S(1)}, bf16[64,4,256]{2,1,0:T(4,128)(2,1)S(1)}, u32[]{:S(2)}, u32[]{:S(2)}) collective-permute-start(bf16[64,4,256]{2,1,0:T(4,128)(2,1)S(1)} %get-tuple-element.20), channel_id=1, source_target_pairs={{1,0},{2,1},{3,2},{4,3},{5,4},{6,5},{7,6},{8,7},{9,8},{10,9},{11,1... | collective-permute-start | bytes 393224 | tf_op jit(solution)/shard_map/ppermute | solution.py:33
  8.0 26.0 %copy-start.2 = (s32[12,27]{1,0:T(8,128)S(1)}, s32[12,27]{1,0:T(8,128)}, u32[]{:S(2)}) copy-start(s32[12,27]{1,0:T(8,128)} %param.7) | copy-start | bytes 3892
  47.0 3.9 %collective-permute-start.2 = (bf16[64,4,128]{2,1,0:T(4,128)(2,1)S(1)}, bf16[64,4,128]{2,1,0:T(4,128)(2,1)S(1)}, u32[]{:S(2)}, u32[]{:S(2)}) collective-permute-start(bf16[64,4,128]{2,1,0:T(4,128)(2,1)S(1)} %get-tuple-element.21), channel_id=1, source_target_pairs={{0,1},{1,2},{2,3},{3,4},{4,5},{5,6},{6,7},{7,8},{8,9},{9,10},{10,1... | collective-permute-start | bytes 196616 | tf_op jit(solution)/shard_map/ppermute | solution.py:32
  49.3 3.1 %collective-permute-start.3 = (bf16[64,4,128]{2,1,0:T(4,128)(2,1)S(1)}, bf16[64,4,128]{2,1,0:T(4,128)(2,1)S(1)}, u32[]{:S(2)}, u32[]{:S(2)}) collective-permute-start(bf16[64,4,128]{2,1,0:T(4,128)(2,1)S(1)} %get-tuple-element.22), channel_id=1, source_target_pairs={{1,0},{2,1},{3,2},{4,3},{5,4},{6,5},{7,6},{8,7},{9,8},{10,9},{11,1... | collective-permute-start | bytes 196616 | tf_op jit(solution)/shard_map/ppermute | solution.py:33

commit v6 on v5

--- a/solution.py
+++ b/solution.py
@@ -241,7 +241,7 @@
 
 def kernel_gradient(win, cots, term):
     channels = term.shape[1]
-    wide = 3 * channels
+    wide = 9 * channels
 
     def step(i, carry):
         columns = pl.ds(pl.multiple_of(i * wide, wide), wide)

time: 88.6 us -> 85.9 us (0.970)
  Pallas kernels: 70.6 us -> 67.9 us
    pallas_call x2, Pallas kernels: 19 us -> 16.4 us  [local_call(): pl.pallas_call(body, out_shape=[jax.ShapeDtypeStruct((rows, channels), jn...]
  transfers between devices with their start and end apart: 4 -> 4, of which waited for: 1 -> 1; matrix products, arithmetic and copies ran while one was open for 1% -> 1% of each run, Pallas kernels for 29% -> 30%
where the time goes in v6:
time: 85.9 us; the launch traced here: 85.6 us
  Pallas kernels  67.9 us (79%)
  starting transfers between devices  7.27 us (8%)
  local copies, waits for them, and re-layouts  5.12 us (6%)
  other arithmetic  2.87 us (3%)
  waiting for transfers between devices  1.54 us (2%)
  between operations  0.89 us (1%)
    pallas_call x1, Pallas kernels, gather_both(): pl.pallas_call(functools.partial(doubling_kernel, size, bit_orders(size))...  25.9 us
    pallas_call x1, Pallas kernels, reduce_both(): pl.pallas_call(functools.partial(halving_kernel, size, bit_orders(size)),...  25.7 us
    pallas_call x2, Pallas kernels, local_call(): pl.pallas_call(body, out_shape=[jax.ShapeDtypeStruct((rows, channels), jn...  16.4 us
    ppermute x2, starting transfers between devices, neighbours(): before = lax.ppermute(packed[:, rim_count:], 'tx', up)  4.69 us
    unnamed x9, local copies, waits for them, and re-layouts  2.9 us
    ppermute x2, starting transfers between devices, neighbours(): after = lax.ppermute(packed[:, :rim_count], 'tx', down)  2.58 us
  transfers between devices with their start and end apart: 4, of which 1 were waited for; matrix products, arithmetic and copies ran while one was open for 1% of the time, Pallas kernels for 30%

profile of v6, /device:TPU:0, one launch (start us, length us, event | category | flops | bytes accessed | tf_op | source)
XLA Modules:
  0.0 85.6 jit_solution(7572717510228787616)
XLA Ops:
  0.6 0.0 copy-start
  0.6 0.0 copy-start.1
  0.7 1.1 %copy.13 = bf16[12,64,128]{2,0,1:T(8,128)(2,1)S(1)} copy(bf16[12,64,128]{2,1,0:T(8,128)(2,1)} %param.6) | data formatting | bytes 393216 | tf_op args[0]
  1.7 1.1 %copy.14 = bf16[12,64,128]{2,0,1:T(8,128)(2,1)S(1)} copy(bf16[12,64,128]{2,1,0:T(8,128)(2,1)} %param.11) | data formatting | bytes 393216 | tf_op args[5]
  2.8 0.7 iota_compare_fusion.1
  3.5 0.1 maximum_bitcast_fusion
  3.6 0.6 select_reduce_fusion
  4.2 0.1 fusion.1
  4.3 2.4 %collective-permute-start = (bf16[64,4,256]{2,1,0:T(4,128)(2,1)S(1)}, bf16[64,4,256]{2,1,0:T(4,128)(2,1)S(1)}, u32[]{:S(2)}, u32[]{:S(2)}) collective-permute-start(bf16[64,4,256]{2,1,0:T(4,128)(2,1)S(1)} %get-tuple-element.19), channel_id=1, source_target_pairs={{0,1},{1,2},{2,3},{3,4},{4,5},{5,6},{6,7},{7,8},{8,9},{9,10},{10,1... | collective-permute-start | bytes 393224 | tf_op jit(solution)/shard_map/ppermute | solution.py:32
  6.6 1.3 %collective-permute-start.1 = (bf16[64,4,256]{2,1,0:T(4,128)(2,1)S(1)}, bf16[64,4,256]{2,1,0:T(4,128)(2,1)S(1)}, u32[]{:S(2)}, u32[]{:S(2)}) collective-permute-start(bf16[64,4,256]{2,1,0:T(4,128)(2,1)S(1)} %get-tuple-element.20), channel_id=1, source_target_pairs={{1,0},{2,1},{3,2},{4,3},{5,4},{6,5},{7,6},{8,7},{9,8},{10,9},{11,1... | collective-permute-start | bytes 393224 | tf_op jit(solution)/shard_map/ppermute | solution.py:33
  7.9 0.0 copy-done
  8.0 0.0 copy-done.1
  8.0 0.0 copy-start.2
  8.0 25.9 %shard_map.85 = (bf16[16,224,128]{2,1,0:T(8,128)(2,1)S(1)}, bf16[16,224,128]{2,1,0:T(8,128)(2,1)S(1)}) custom-call(bf16[224,128]{1,0:T(8,128)(2,1)S(1)} %pad.23.first, bf16[224,128]{1,0:T(8,128)(2,1)S(1)} %pad.24.second), custom_call_target="tpu_custom_call" | custom-call | tf_op jit(solution)/shard_map/pallas_call | solution.py:178
  33.9 0.1 slice.35
  34.0 0.1 slice.36
  34.0 0.0 copy-done.2
  34.0 0.1 copy.15
  34.1 0.1 pad.37.clone
  34.2 0.2 pad_maximum_fusion.both_w
  34.4 0.1 fusion.choose
  34.5 0.0 collective-permute-done
  34.6 0.0 collective-permute-done.1
  34.6 0.5 maximum_maximum_fusion.extended
  35.1 10.0 %shard_map.86 = (bf16[1024,128]{1,0:T(8,128)(2,1)S(1)}, f32[3456,128]{1,0:T(8,128)S(1)}) custom-call(bf16[64,32,256]{2,1,0:T(8,128)(2,1)S(1)} %maximum_maximum_fusion.extended, bf16[27,16,32]{2,1,0:T(8,128)(2,1)S(1)} %fusion.choose, bf16[3456,256]{1,0:T(8,128)(2,1)S(1)} %pad_maximum_fusion.both_w), custom_call_target="tpu_custom_call" | custom-call | tf_op jit(solution)/shard_map/pallas_call | solution.py:315
  45.1 0.5 select_reduce_fusion.1
  45.7 2.3 %collective-permute-start.2 = (bf16[64,4,128]{2,1,0:T(4,128)(2,1)S(1)}, bf16[64,4,128]{2,1,0:T(4,128)(2,1)S(1)}, u32[]{:S(2)}, u32[]{:S(2)}) collective-permute-start(bf16[64,4,128]{2,1,0:T(4,128)(2,1)S(1)} %get-tuple-element.21), channel_id=1, source_target_pairs={{0,1},{1,2},{2,3},{3,4},{4,5},{5,6},{6,7},{7,8},{8,9},{9,10},{10,1... | collective-permute-start | bytes 196616 | tf_op jit(solution)/shard_map/ppermute | solution.py:32
  48.0 1.3 %collective-permute-start.3 = (bf16[64,4,128]{2,1,0:T(4,128)(2,1)S(1)}, bf16[64,4,128]{2,1,0:T(4,128)(2,1)S(1)}, u32[]{:S(2)}, u32[]{:S(2)}) collective-permute-start(bf16[64,4,128]{2,1,0:T(4,128)(2,1)S(1)} %get-tuple-element.22), channel_id=1, source_target_pairs={{1,0},{2,1},{3,2},{4,3},{5,4},{6,5},{7,6},{8,7},{9,8},{10,9},{11,1... | collective-permute-start | bytes 196616 | tf_op jit(solution)/shard_map/ppermute | solution.py:33
  49.4 0.1 pad.25
  49.4 0.2 pad.26.first
  49.6 0.0 collective-permute-done.2
  49.6 1.5 %collective-permute-done.3 = bf16[64,4,128]{2,1,0:T(4,128)(2,1)S(1)} collective-permute-done((bf16[64,4,128]{2,1,0:T(4,128)(2,1)S(1)}, bf16[64,4,128]{2,1,0:T(4,128)(2,1)S(1)}, u32[]{:S(2)}, u32[]{:S(2)}) %collective-permute-start.3) | collective-permute-done | bytes 65568 | tf_op jit(solution)/shard_map/ppermute | solution.py:33
  51.2 0.2 maximum_maximum_fusion.1.extended
  51.4 6.3 %shard_map.87 = (bf16[1024,128]{1,0:T(8,128)(2,1)S(1)}, f32[3456,128]{1,0:T(8,128)S(1)}) custom-call(bf16[64,32,128]{2,1,0:T(8,128)(2,1)S(1)} %maximum_maximum_fusion.1.extended, bf16[1024,128]{1,0:T(8,128)(2,1)S(1)} %bitcast.21, bf16[3456,256]{1,0:T(8,128)(2,1)S(1)} %pad_maximum_fusion.both_w, bf16[27,16,32]{2,1,0:T(8,128)(2,1)S(1)} %fusion.choose), custom_call_target="tpu_custom_call" | custom-call | tf_op jit(solution)/shard_map/pallas_call | solution.py:315
  57.7 0.2 pad.27.second
  57.9 25.7 %shard_map.88 = (f32[224,128]{1,0:T(8,128)S(1)}, f32[224,128]{1,0:T(8,128)S(1)}) custom-call(f32[16,224,128]{2,1,0:T(8,128)S(1)} %pad.26.first, f32[16,224,128]{2,1,0:T(8,128)S(1)} %pad.27.second), custom_call_target="tpu_custom_call" | custom-call | tf_op jit(solution)/shard_map/pallas_call | solution.py:203
  83.6 0.7 slice.42
  84.3 0.7 slice.43
  84.9 0.7 copy.19
  (6 shorter events, 0.1 us)
Async XLA Ops:
  0.6 7.3 %copy-start = (bf16[216,128]{1,0:T(8,128)(2,1)S(1)}, bf16[216,128]{1,0:T(8,128)(2,1)}, u32[]{:S(2)}) copy-start(bf16[216,128]{1,0:T(8,128)(2,1)} %param.9) | copy-start | bytes 165892
  0.6 7.3 %copy-start.1 = (bf16[216,128]{1,0:T(8,128)(2,1)S(1)}, bf16[216,128]{1,0:T(8,128)(2,1)}, u32[]{:S(2)}) copy-start(bf16[216,128]{1,0:T(8,128)(2,1)} %param.10) | copy-start | bytes 165892
  4.3 30.3 %collective-permute-start = (bf16[64,4,256]{2,1,0:T(4,128)(2,1)S(1)}, bf16[64,4,256]{2,1,0:T(4,128)(2,1)S(1)}, u32[]{:S(2)}, u32[]{:S(2)}) collective-permute-start(bf16[64,4,256]{2,1,0:T(4,128)(2,1)S(1)} %get-tuple-element.19), channel_id=1, source_target_pairs={{0,1},{1,2},{2,3},{3,4},{4,5},{5,6},{6,7},{7,8},{8,9},{9,10},{10,1... | collective-permute-start | bytes 393224 | tf_op jit(solution)/shard_map/ppermute | solution.py:32
  6.6 27.9 %collective-permute-start.1 = (bf16[64,4,256]{2,1,0:T(4,128)(2,1)S(1)}, bf16[64,4,256]{2,1,0:T(4,128)(2,1)S(1)}, u32[]{:S(2)}, u32[]{:S(2)}) collective-permute-start(bf16[64,4,256]{2,1,0:T(4,128)(2,1)S(1)} %get-tuple-element.20), channel_id=1, source_target_pairs={{1,0},{2,1},{3,2},{4,3},{5,4},{6,5},{7,6},{8,7},{9,8},{10,9},{11,1... | collective-permute-start | bytes 393224 | tf_op jit(solution)/shard_map/ppermute | solution.py:33
  8.0 26.0 %copy-start.2 = (s32[12,27]{1,0:T(8,128)S(1)}, s32[12,27]{1,0:T(8,128)}, u32[]{:S(2)}) copy-start(s32[12,27]{1,0:T(8,128)} %param.7) | copy-start | bytes 3892
  45.7 3.9 %collective-permute-start.2 = (bf16[64,4,128]{2,1,0:T(4,128)(2,1)S(1)}, bf16[64,4,128]{2,1,0:T(4,128)(2,1)S(1)}, u32[]{:S(2)}, u32[]{:S(2)}) collective-permute-start(bf16[64,4,128]{2,1,0:T(4,128)(2,1)S(1)} %get-tuple-element.21), channel_id=1, source_target_pairs={{0,1},{1,2},{2,3},{3,4},{4,5},{5,6},{6,7},{7,8},{8,9},{9,10},{10,1... | collective-permute-start | bytes 196616 | tf_op jit(solution)/shard_map/ppermute | solution.py:32
  48.0 3.1 %collective-permute-start.3 = (bf16[64,4,128]{2,1,0:T(4,128)(2,1)S(1)}, bf16[64,4,128]{2,1,0:T(4,128)(2,1)S(1)}, u32[]{:S(2)}, u32[]{:S(2)}) collective-permute-start(bf16[64,4,128]{2,1,0:T(4,128)(2,1)S(1)} %get-tuple-element.22), channel_id=1, source_target_pairs={{1,0},{2,1},{3,2},{4,3},{5,4},{6,5},{7,6},{8,7},{9,8},{10,9},{11,1... | collective-permute-start | bytes 196616 | tf_op jit(solution)/shard_map/ppermute | solution.py:33
